TPU v7x, 128 devices: a whole 4x4x4 slice. The times are simulated.
128 devices in a mesh: table: 32 (over x, y, core), blk: 4 (over z).
Axes of the slice: x: 4, y: 4, z: 4, core: 2. Of those that a mesh axis runs over, the one named last changes fastest.
Arguments:
- entity_table: bfloat16 [524288, 400], P(('table', 'blk')), may hold values from -6 to 6
- rel_center: bfloat16 [7424, 400], replicated, may hold values from -3 to 3
- rel_offset: bfloat16 [7424, 400], replicated, may hold values from -6 to 6
- entity_owner: int32 [32768, 2, 1], P(('table', 'blk')), may hold values from 0 to 127; in each aligned block of 512 rows (0 to 511, 512 to 1023, ..., all dimensions but the last counted through in order) at most 8 rows name the same one
- entity_row: int32 [32768, 2], P(('table', 'blk')), may hold values from 0 to 4095
- rel_ids: int32 [32768, 3], P(('table', 'blk')), may hold values from 0 to 7423
- query_type: int32 [32768], P(('table', 'blk')), may hold values from 0 to 2
- neg_rows: int32 [4096], P(('table', 'blk')), may hold values from 0 to 4095
Outputs:
- entity_grad: float32 [524288, 400], P(('table', 'blk'))
Inputs may be any that keep to these rules, and one draw needn't show every extreme that they name: `entity_owner`: among the 512 anchor and answer entries of one device no owner is named more than 8 times; in some devices' entries an owner is named exactly 8 times.
All inputs are finite; a program needn't handle non-finite values.
Results may differ from a plain program's by a relative error of at most 0.0003.
Values may be sent and summed in bfloat16 or wider, within the bound.
A program may use at most 128 MiB of HBM per device.

v0:
```python
import functools
import math
import jax
import jax.numpy as jnp
from jax import lax
from jax.experimental import pallas as pl
from jax.experimental.pallas import tpu as pltpu
from jax.sharding import PartitionSpec as P

margin_gamma = 7.0
dist_scale = 0.02
inside_weight = 0.2
smooth_eps = 0.01
loss_scale = 64.0

f32 = jnp.float32
bf16 = jnp.bfloat16
i32 = jnp.int32
log2e = math.log2(math.e)
scaled_eps = smooth_eps * log2e * log2e
dist_unit = dist_scale * math.log(2.0) * inside_weight
log_weight = (1.0 - inside_weight) / inside_weight
slope_weight = 1.0 - inside_weight
lanes = 128
near = 8


def iota(shape, axis):
    return lax.broadcasted_iota(i32, shape, axis)


def dot(a, b, ca, cb):
    return lax.dot_general(a, b, (((ca,), (cb,)), ((), ())), preferred_element_type=f32)


def whole():
    return pl.BlockSpec(memory_space=pltpu.VMEM)


def params(mib, **more):
    return pltpu.CompilerParams(vmem_limit_bytes=mib * 2**20, **more)


def shifted(value, axis, steps):
    count = lax.axis_size(axis)
    pairs = [(source, (source + steps) % count) for source in range(count)]
    return lax.ppermute(value, axis, pairs)


def one_hot(mask):
    return jnp.where(mask, 1.0, 0.0).astype(bf16)


def slots_kernel(slot_count, devices, owner_ref, row_ref, wanted_ref, slot_ref):
    owner = jnp.concatenate([owner_ref[0:1, :], owner_ref[1:2, :]], axis=1)
    row = jnp.concatenate([row_ref[0:1, :], row_ref[1:2, :]], axis=1)
    requests = owner.shape[1]
    named = iota((devices, requests), 0) == owner
    named_hot = one_hot(named)
    earlier = one_hot(iota((requests, requests), 0) < iota((requests, requests), 1))
    before = dot(named_hot, earlier, 1, 0)
    rank = jnp.sum(jnp.where(named, before, 0.0), axis=0, keepdims=True).astype(i32)
    slot_ref[...] = owner * slot_count + rank
    high = lax.shift_right_logical(row, 6)
    low = row - high * 64
    ranked = iota((lanes, requests), 0) == rank
    high_hot = jnp.where(ranked, high.astype(f32), 0.0).astype(bf16)
    low_hot = jnp.where(ranked, low.astype(f32), 0.0).astype(bf16)
    asked = dot(named_hot, high_hot, 1, 1) * 64.0 + dot(named_hot, low_hot, 1, 1)
    wanted_ref[...] = asked.astype(i32)


def plan_slots(owner, row, slot_count, devices):
    requests = owner.shape[0] * owner.shape[1]
    return pl.pallas_call(
        functools.partial(slots_kernel, slot_count, devices),
        out_shape=(
            jax.ShapeDtypeStruct((devices, lanes), i32),
            jax.ShapeDtypeStruct((1, requests), i32),
        ),
        in_specs=[whole(), whole()],
        out_specs=(whole(), whole()),
        compiler_params=params(32),
        name="plan_slots",
    )(owner, row)


def asked_column(asked, slot_count):
    devices = asked.shape[0]
    rows = devices * slot_count
    high = lax.shift_right_logical(asked, 6)
    low = asked - high * 64
    group = lax.shift_right_logical(iota((rows, devices), 0), int(math.log2(slot_count)))
    pick = one_hot(group == iota((rows, devices), 1))
    spread = dot(pick, high.astype(f32).astype(bf16), 1, 0) * 64.0 + dot(
        pick, low.astype(f32).astype(bf16), 1, 0
    )
    mine = (iota((rows, lanes), 0) & (slot_count - 1)) == iota((rows, lanes), 1)
    return jnp.sum(jnp.where(mine, spread, 0.0), axis=1, keepdims=True).astype(i32)


def serve_kernel(slot_count, asked_ref, neg_ref, table_ref, served_ref, pool_ref, total, column):
    step = pl.program_id(0)
    part = table_ref.shape[1]
    rows = served_ref.shape[0]
    pool = pool_ref.shape[0]

    @pl.when(step == 0)
    def _():
        column[0:rows, :] = asked_column(asked_ref[...], slot_count)
        here = iota((pool, pool), 0) == iota((pool, pool), 1)
        column[rows : rows + pool, :] = jnp.sum(
            jnp.where(here, neg_ref[...].astype(f32), 0.0), axis=1, keepdims=True
        ).astype(i32)
        total[...] = jnp.zeros_like(total)

    base = step * part
    for start in range(0, rows + pool, 256):
        size = min(256, rows + pool - start)
        block = pl.ds(start, size)
        hot = one_hot(iota((size, part), 1) + base == column[block, :])
        total[block, :] += dot(hot, table_ref[...], 1, 1)

    @pl.when(step == pl.num_programs(0) - 1)
    def _():
        served_ref[...] = total[0:rows, :].astype(bf16)
        pool_ref[...] = total[rows : rows + pool, :].astype(bf16)


def serve(asked, neg_rows, table, slot_count):
    width, entities = table.shape
    rows = asked.shape[0] * slot_count
    pool = neg_rows.shape[1]
    part = 1024
    return pl.pallas_call(
        functools.partial(serve_kernel, slot_count),
        out_shape=(
            jax.ShapeDtypeStruct((rows, width), bf16),
            jax.ShapeDtypeStruct((pool, width), bf16),
        ),
        grid=(entities // part,),
        in_specs=[
            pl.BlockSpec(asked.shape, lambda i: (0, 0)),
            pl.BlockSpec(neg_rows.shape, lambda i: (0, 0)),
            pl.BlockSpec((width, part), lambda i: (0, i)),
        ],
        out_specs=(
            pl.BlockSpec((rows, width), lambda i: (0, 0)),
            pl.BlockSpec((pool, width), lambda i: (0, 0)),
        ),
        scratch_shapes=[pltpu.VMEM((rows + pool, width), f32), pltpu.VMEM((rows + pool, 1), i32)],
        compiler_params=params(40),
        cost_estimate=pl.CostEstimate(
            flops=2 * (rows + pool) * width * entities,
            bytes_accessed=2 * width * entities,
            transcendentals=0,
        ),
        name="serve",
    )(asked, neg_rows, table)


def softplus(x):
    return jnp.maximum(x, 0.0) + jnp.log1p(jnp.exp(-jnp.abs(x)))


def relations_kernel(ids_ref, type_ref, center_hbm, offset_hbm, shift_ref, size_ref,
                     center_tab, offset_tab, center_sum, offset_rows, sems):
    hops, queries = ids_ref.shape
    width, rels = center_tab.shape
    copies = [
        pltpu.make_async_copy(center_hbm, center_tab, sems.at[0]),
        pltpu.make_async_copy(offset_hbm, offset_tab, sems.at[1]),
    ]
    for copy in copies:
        copy.start()
    center_sum[...] = jnp.zeros_like(center_sum)
    offset_rows[...] = jnp.zeros_like(offset_rows)
    for copy in copies:
        copy.wait()

    def part(base, size):
        columns = pl.ds(base, size)
        count = jnp.zeros((size, queries), f32)
        hots = []
        for hop in range(hops):
            hot = jnp.where(iota((size, queries), 0) + base == ids_ref[hop : hop + 1, :], 1.0, 0.0)
            hots.append(hot.astype(bf16))
            count = count + jnp.where(type_ref[...] >= hop, hot, 0.0)
        center_sum[...] += dot(center_tab[:, columns], count.astype(bf16), 1, 0)
        for hop in range(hops):
            here = pl.ds(hop * queries, queries)
            offset_rows[:, here] += dot(offset_tab[:, columns], hots[hop], 1, 0)

    step = 1024

    def body(i, _):
        part(pl.multiple_of(i * step, step), step)
        return 0

    lax.fori_loop(0, rels // step, body, 0)
    if rels % step:
        part(rels // step * step, rels % step)
    shift_ref[...] = center_sum[...]
    total = jnp.zeros((width, queries), f32)
    for hop in range(hops):
        value = softplus(offset_rows[:, hop * queries : (hop + 1) * queries])
        total = total + jnp.where(type_ref[...] >= hop, value, 0.0)
    size_ref[...] = total


def relations(rel_ids, query_type, rel_center, rel_offset):
    hops, queries = rel_ids.shape
    width, rels = rel_center.shape
    return pl.pallas_call(
        relations_kernel,
        out_shape=(
            jax.ShapeDtypeStruct((width, queries), f32),
            jax.ShapeDtypeStruct((width, queries), f32),
        ),
        in_specs=[whole(), whole(), pl.BlockSpec(memory_space=pl.ANY),
                  pl.BlockSpec(memory_space=pl.ANY)],
        out_specs=(whole(), whole()),
        scratch_shapes=[
            pltpu.VMEM((width, rels), bf16),
            pltpu.VMEM((width, rels), bf16),
            pltpu.VMEM((width, queries), f32),
            pltpu.VMEM((width, hops * queries), f32),
            pltpu.SemaphoreType.DMA((2,)),
        ],
        compiler_params=params(48),
        cost_estimate=pl.CostEstimate(
            flops=2 * (hops + 1) * queries * width * rels,
            bytes_accessed=4 * width * rels,
            transcendentals=0,
        ),
        name="relations",
    )(rel_ids, query_type, rel_center, rel_offset)


def slope_terms(gap, size):
    square = gap * gap + scaled_eps
    inverse = lax.rsqrt(square)
    spread = square * inverse
    above = 1.0 + jnp.exp2(spread - size)
    slope = (1.0 - slope_weight * pl.reciprocal(above, approx=True)) * (gap * inverse)
    return spread, above, slope


def grads_kernel(slot_ref, back_ref, shift_ref, size_ref, p0, p1, p2, p3, slots_ref, pool_ref,
                 entity, spread_out, center, size, grads, slopes, dists, weights, pool_grad):
    width, queries = shift_ref.shape
    rows = back_ref.shape[0]
    pool = p0.shape[0]
    negatives = 4 * pool
    tiles = width // 8

    hot = one_hot(iota((rows, 2 * queries), 0) == slot_ref[...])
    picked = dot(back_ref[...], hot, 0, 0)
    center[...] = (picked[:, 0:queries] + shift_ref[...]) * log2e
    size[...] = size_ref[...] * log2e
    grads[:, queries:] = picked[:, queries:] * log2e
    blocks = jnp.concatenate([p0[...], p1[...], p2[...], p3[...]], axis=0)
    eye = one_hot(iota((negatives, negatives), 0) == iota((negatives, negatives), 1))
    columns = dot(blocks, eye, 0, 0) * log2e
    high = columns.astype(bf16)
    entity[:, 0:negatives] = high
    entity[:, negatives:] = (columns - high.astype(f32)).astype(bf16)
    pool_grad[...] = jnp.zeros_like(pool_grad)

    spread, above, slope = slope_terms(grads[:, queries:] - center[...], size[...])
    total = jnp.sum(spread + log_weight * jnp.log2(above), axis=0, keepdims=True) * dist_unit
    weight = (loss_scale * dist_scale) / (1.0 + jnp.exp(margin_gamma - total))
    slope = slope * weight
    grads[:, 0:queries] = -slope
    grads[:, queries:] = slope

    halves = [pl.ds(half * lanes, lanes) for half in range(queries // lanes)]
    lane = iota((8, lanes), 1)
    group = 4
    block = 10

    def chunk(j, _):
        here = j * near
        picks = iota((2 * negatives, near * lanes), 0) & (negatives - 1)
        picks = one_hot(picks == here + lax.shift_right_logical(iota(picks.shape, 1), 7))
        spread_out[...] = dot(entity[...], picks, 1, 0)
        for first in range(0, near, group):
            def forward(base, count, sums):
                sums = list(sums)
                for k in range(group):
                    at = first + k
                    for half, ql in enumerate(halves):
                        product = None
                        total = sums[half * group + k]
                        for tile in range(count):
                            d = pl.ds(base + tile * 8, 8)
                            column = spread_out[d, at * lanes : (at + 1) * lanes]
                            spread, above, slope = slope_terms(column - center[d, ql], size[d, ql])
                            slopes[at, d, ql] = slope
                            product = above if product is None else product * above
                            total = total + spread
                        sums[half * group + k] = total + log_weight * jnp.log2(product)
                return tuple(sums)

            sums = tuple(jnp.zeros((8, lanes), f32) for _ in range(group * len(halves)))
            sums = lax.fori_loop(
                0, tiles // 4, lambda i, s: forward(pl.multiple_of(i * 32, 32), 4, s), sums
            )
            if tiles % 4:
                sums = forward(tiles // 4 * 32, tiles % 4, sums)
            for half, ql in enumerate(halves):
                for k in range(group):
                    dists[first + k : first + k + 1, ql] = jnp.sum(
                        sums[half * group + k], axis=0, keepdims=True
                    )
        scale = -loss_scale * dist_scale / negatives
        weights[...] = scale / (1.0 + jnp.exp(dists[...] * dist_unit - margin_gamma))
        weight_rows = [
            [jnp.broadcast_to(weights[k : k + 1, ql], (8, lanes)) for ql in halves]
            for k in range(near)
        ]

        def backward(i, _):
            for tile in range(block):
                d = pl.ds(pl.multiple_of(i * (8 * block), 8) + tile * 8, 8)
                to_center = [grads[d, ql] for ql in halves]
                to_pool = pool_grad[d, :]
                for k in range(near):
                    row = None
                    for half, ql in enumerate(halves):
                        term = slopes[k, d, ql] * weight_rows[k][half]
                        to_center[half] = to_center[half] - term
                        row = term if row is None else row + term
                    row = jnp.sum(row, axis=1, keepdims=True)
                    to_pool = jnp.where(lane == here + k, row, to_pool)
                for half, ql in enumerate(halves):
                    grads[d, ql] = to_center[half]
                pool_grad[d, :] = to_pool
            return 0

        lax.fori_loop(0, tiles // block, backward, 0)
        return 0

    lax.fori_loop(0, negatives // near, chunk, 0)

    value = grads[...]
    high = value.astype(bf16)
    low = (value - high.astype(f32)).astype(bf16)
    slots_ref[...] = dot(hot, high, 1, 1) + dot(hot, low, 1, 1)
    pool_ref[...] = jnp.transpose(pool_grad[...])[:, 0:width]


def gradients(slot, back, shift, size, blocks):
    width, queries = shift.shape
    rows = back.shape[0]
    pool = blocks[0].shape[0]
    negatives = 4 * pool
    padded = -(-width // lanes) * lanes
    work = negatives * queries * width
    return pl.pallas_call(
        grads_kernel,
        out_shape=(
            jax.ShapeDtypeStruct((rows, width), f32),
            jax.ShapeDtypeStruct((negatives, width), f32),
        ),
        in_specs=[whole()] * 8,
        out_specs=(whole(), whole()),
        scratch_shapes=[
            pltpu.VMEM((width, 2 * negatives), bf16),
            pltpu.VMEM((width, near * lanes), f32),
            pltpu.VMEM((width, queries), f32),
            pltpu.VMEM((width, queries), f32),
            pltpu.VMEM((width, 2 * queries), f32),
            pltpu.VMEM((near, width, queries), f32),
            pltpu.VMEM((near, queries), f32),
            pltpu.VMEM((near, queries), f32),
            pltpu.VMEM((padded, negatives), f32),
        ],
        compiler_params=params(48),
        cost_estimate=pl.CostEstimate(
            flops=16 * work, bytes_accessed=4 * rows * width, transcendentals=3 * work
        ),
        name="gradients",
    )(slot, back, shift, size, *blocks)


def scatter_kernel(slot_count, asked_ref, neg_ref, back_ref, own_ref, q1, q2, q3, out_ref, column, both):
    step = pl.program_id(0)
    part = out_ref.shape[1]
    rows, width = back_ref.shape
    pool = q1.shape[0]

    @pl.when(step == 0)
    def _():
        column[0:rows, :] = asked_column(asked_ref[...], slot_count)
        here = iota((pool, pool), 0) == iota((pool, pool), 1)
        column[rows:, :] = jnp.sum(
            jnp.where(here, neg_ref[...].astype(f32), 0.0), axis=1, keepdims=True
        ).astype(i32)

        def place(value, start):
            size = value.shape[0]
            high = value.astype(bf16)
            low = (value - high.astype(f32)).astype(bf16)
            both[start : start + size, 0:width] = high
            both[start : start + size, 512 : 512 + width] = low

        both[...] = jnp.zeros_like(both)
        place(back_ref[...], 0)
        place(own_ref[...] + q1[...] + q2[...] + q3[...], rows)

    hot = one_hot(iota((rows + pool, part), 1) + step * part == column[...])
    result = dot(both[...], hot, 0, 0)
    out_ref[...] = result[0:width, :] + result[512 : 512 + width, :]


def scatter(asked, neg_rows, back, own, others, slot_count, entities):
    rows, width = back.shape
    pool = own.shape[0]
    part = 512
    fixed = lambda i: (0, 0)
    return pl.pallas_call(
        functools.partial(scatter_kernel, slot_count),
        out_shape=jax.ShapeDtypeStruct((width, entities), f32),
        grid=(entities // part,),
        in_specs=[
            pl.BlockSpec(asked.shape, fixed),
            pl.BlockSpec(neg_rows.shape, fixed),
            pl.BlockSpec((rows, width), fixed),
        ]
        + [pl.BlockSpec((pool, width), fixed)] * 4,
        out_specs=pl.BlockSpec((width, part), lambda i: (0, i)),
        scratch_shapes=[pltpu.VMEM((rows + pool, 1), i32), pltpu.VMEM((rows + pool, 1024), bf16)],
        compiler_params=params(48),
        name="scatter",
    )(asked, neg_rows, back, own, *others)


def local(
    entity_table, rel_center, rel_offset, entity_owner, entity_row, rel_ids, query_type, neg_rows
):
    entities, width = entity_table.shape
    table_size = lax.axis_size("table")
    group_size = lax.axis_size("blk")
    devices = table_size * group_size
    queries = rel_ids.shape[0]
    slot_count = 4 * queries // devices
    pool = neg_rows.shape[0]
    axes = ("table", "blk")
    exchange = functools.partial(
        lax.all_to_all, axis_name=axes, split_axis=0, concat_axis=0, tiled=True
    )
    table = entity_table.T
    neg_row = neg_rows.reshape(1, pool)
    wanted, slot = plan_slots(
        entity_owner[:, :, 0].T, entity_row.T, slot_count, devices
    )
    asked = exchange(wanted.reshape(devices, 1, lanes)).reshape(devices, lanes)
    served, block = serve(asked, neg_row, table, slot_count)
    back = exchange(served.reshape(devices, slot_count, width)).reshape(-1, width)
    shift, size = relations(rel_ids.T, query_type.reshape(1, queries), rel_center.T, rel_offset.T)
    blocks = [block] + [shifted(block, "blk", step) for step in range(1, group_size)]
    slot_grads, pool_grads = gradients(slot, back, shift, size, blocks)
    returned = exchange(slot_grads.reshape(devices, slot_count, width)).reshape(-1, width)
    others = [
        shifted(pool_grads[step * pool : (step + 1) * pool], "blk", -step)
        for step in range(1, group_size)
    ]
    return scatter(
        asked, neg_row, returned, pool_grads[0:pool], others, slot_count, entities
    ).T


def solution(mesh):
    placed = (
        P(("table", "blk"), None),
        P(),
        P(),
        P(("table", "blk"), None, None),
        P(("table", "blk"), None),
        P(("table", "blk"), None),
        P(("table", "blk")),
        P(("table", "blk")),
    )
    return jax.shard_map(
        local, mesh=mesh, in_specs=placed, out_specs=P(("table", "blk"), None), check_vma=False
    )
```

profile of v0, /device:TPU:1, one launch (start us, length us, event | category | flops | bytes accessed | tf_op | source)
XLA Modules:
  0.0 171.9 jit_solution(2856006621972756939)
XLA Ops:
  0.0 0.7 copy.12
  0.7 0.0 copy-start.1
  0.7 0.7 copy-done.1
  1.4 0.5 plan_slots.1
  1.8 21.0 %all_to_all.15 = s32[128,1,128]{2,1,0:T(1,128)S(1)} all-to-all(s32[128,1,128]{2,1,0:T(1,128)S(1)} %bitcast.26), channel_id=1, replica_groups=mesh['table'=32,'blk'=4] {'table','blk'}, dimensions={0} | all-to-all | bytes 131072 | tf_op jit(solution)/shard_map/all_to_all | solution.py:458
  22.8 0.7 copy-done.2
  23.5 1.9 %copy-done.4 = bf16[4096,400]{0,1:T(8,128)(2,1)S(1)} copy-done((bf16[4096,400]{0,1:T(8,128)(2,1)S(1)}, bf16[4096,400]{0,1:T(8,128)(2,1)}, u32[]{:S(2)}) %copy-start.4) | copy-done | bytes 3276824
  25.4 7.8 %serve.1 = (bf16[1024,400]{1,0:T(8,128)(2,1)}, bf16[32,400]{1,0:T(8,128)(2,1)S(1)}) custom-call(s32[128,128]{1,0:T(8,128)S(1)} %bitcast.24, s32[1,32]{1,0:T(1,128)S(1)} %bitcast.29, bf16[400,4096]{1,0:T(8,128)(2,1)S(1)} %bitcast.31), custom_call_target="tpu_custom_call" | custom-call | flops 3460300800 | bytes 3276800 | tf_op jit(solution)/shard_map/serve/pallas_call | solution.py:135
  33.2 4.3 %all-to-all-start.1 = ((bf16[128,8,400]{2,1,0:T(8,128)(2,1)}), bf16[128,8,400]{2,1,0:T(8,128)(2,1)S(1)}, u32[]{:S(2)}, u32[]{:S(2)}) async-start(bf16[128,8,400]{2,1,0:T(8,128)(2,1)} %bitcast.7), calls=%async_computation.1 | async-start | bytes 2097152 | tf_op jit(solution)/shard_map/all_to_all | solution.py:460
  37.4 3.3 %collective-permute-start.2 = (bf16[32,400]{1,0:T(8,128)(2,1)S(1)}, bf16[32,400]{1,0:T(8,128)(2,1)S(1)}, u32[]{:S(2)}, u32[]{:S(2)}) collective-permute-start(bf16[32,400]{1,0:T(8,128)(2,1)S(1)} %get-tuple-element.18.p0), channel_id=1, source_target_pairs={{0,3},{1,0},{2,1},{3,2},{4,7},{5,4},{6,5},{7,6},{8,11},{9,8},{10,9... | collective-permute-start | bytes 76808 | tf_op jit(solution)/shard_map/ppermute | solution.py:47
  40.8 0.1 collective-permute-start.1
  40.9 0.8 collective-permute-start
  41.7 0.0 copy-done.5
  41.7 0.0 copy-done.6
  41.7 13.4 %relations.1 = (f32[400,256]{1,0:T(8,128)S(1)}, f32[400,256]{1,0:T(8,128)S(1)}) custom-call(s32[3,256]{1,0:T(4,128)S(1)} %bitcast.32, s32[1,256]{1,0:T(1,128)S(1)} %bitcast.33, bf16[400,7424]{1,0:T(8,128)(2,1)} %bitcast.34, bf16[400,7424]{1,0:T(8,128)(2,1)} %bitcast.35), custom_call_target="tpu_custom_call" | custom-call | flops 6081740800 | bytes 11878400 | tf_op jit(solution)/shard_map/relations/pallas_call | solution.py:214
  55.1 0.0 collective-permute-done.2.p3
  55.1 0.0 collective-permute-done.1.p2
  55.1 0.0 collective-permute-done.p1
  55.2 1.9 %all-to-all-done.1 = bf16[128,8,400]{2,1,0:T(8,128)(2,1)S(1)} async-done(((bf16[128,8,400]{2,1,0:T(8,128)(2,1)}), bf16[128,8,400]{2,1,0:T(8,128)(2,1)S(1)}, u32[]{:S(2)}, u32[]{:S(2)}) %all-to-all-start.1) | async-done | bytes 819232 | tf_op jit(solution)/shard_map/all_to_all | solution.py:460
  57.0 60.5 %gradients.1 = (f32[1024,400]{1,0:T(8,128)S(1)}, f32[128,400]{1,0:T(8,128)S(1)}) custom-call(s32[1,512]{1,0:T(1,128)S(1)} %get-tuple-element.14.slot_ref, bf16[1024,400]{1,0:T(8,128)(2,1)S(1)} %bitcast.23, f32[400,256]{1,0:T(8,128)S(1)} %get-tuple-element.16.shift_ref, f32[400,256]{1,0:T(8,128)S(1)} %get-tuple-element.17.size_ref, ...), custom_call_target="tpu_custom_call" | custom-call | flops 209715200 | bytes 1638400 | tf_op jit(solution)/shard_map/gradients/pallas_call | solution.py:360
  117.6 0.0 copy-start
  117.6 1.3 copy-done
  118.9 7.3 %all-to-all-start.2 = ((f32[128,8,400]{2,1,0:T(8,128)}), f32[128,8,400]{2,1,0:T(8,128)S(1)}, u32[]{:S(2)}, u32[]{:S(2)}) async-start(f32[128,8,400]{2,1,0:T(8,128)} %bitcast.22), calls=%async_computation.2 | async-start | bytes 4194304 | tf_op jit(solution)/shard_map/all_to_all | solution.py:464
  126.2 1.6 collective-permute-start.5
  127.8 2.9 %collective-permute-start.4 = (f32[32,400]{1,0:T(8,128)S(1)}, f32[32,400]{1,0:T(8,128)S(1)}, u32[]{:S(2)}, u32[]{:S(2)}) collective-permute-start(f32[32,400]{1,0:T(8,128)S(1)} %get-tuple-element.22), channel_id=1, source_target_pairs={{0,2},{1,3},{2,0},{3,1},{4,6},{5,7},{6,4},{7,5},{8,10},{9,11},{10,... | collective-permute-start | bytes 153608 | tf_op jit(solution)/shard_map/ppermute | solution.py:47
  130.7 0.9 collective-permute-start.3
  131.6 15.2 %collective-permute-done.5.q3 = f32[32,400]{1,0:T(8,128)S(1)} collective-permute-done((f32[32,400]{1,0:T(8,128)S(1)}, f32[32,400]{1,0:T(8,128)S(1)}, u32[]{:S(2)}, u32[]{:S(2)}) %collective-permute-start.5) | collective-permute-done | bytes 51232 | tf_op jit(solution)/shard_map/ppermute | solution.py:47
  146.8 7.2 %collective-permute-done.4.q2 = f32[32,400]{1,0:T(8,128)S(1)} collective-permute-done((f32[32,400]{1,0:T(8,128)S(1)}, f32[32,400]{1,0:T(8,128)S(1)}, u32[]{:S(2)}, u32[]{:S(2)}) %collective-permute-start.4) | collective-permute-done | bytes 51232 | tf_op jit(solution)/shard_map/ppermute | solution.py:47
  154.0 0.0 collective-permute-done.3.q1
  154.0 3.0 %all-to-all-done.2 = f32[128,8,400]{2,1,0:T(8,128)S(1)} async-done(((f32[128,8,400]{2,1,0:T(8,128)}), f32[128,8,400]{2,1,0:T(8,128)S(1)}, u32[]{:S(2)}, u32[]{:S(2)}) %all-to-all-start.2) | async-done | bytes 1638432 | tf_op jit(solution)/shard_map/all_to_all | solution.py:464
  157.0 0.0 copy-done.3
  157.0 14.9 %scatter.1 = f32[400,4096]{1,0:T(8,128)} custom-call(s32[128,128]{1,0:T(8,128)S(1)} %bitcast.25, s32[1,32]{1,0:T(1,128)S(1)} %bitcast.30, f32[1024,400]{1,0:T(8,128)S(1)} %bitcast.21, f32[32,400]{1,0:T(8,128)S(1)} %get-tuple-element.24.own_ref, f32[32,400]{1,0:T(8,128)S(1)} %collective-permute-done.3.q1, f32[32,400]{1,0:T(8,128)S(1)} %collective-permute-done.4.q2, ...), custom_call_target="tpu_custom_call" | custom-call | tf_op jit(solution)/shard_map/scatter/pallas_call | solution.py:422
  (6 shorter events, 0.0 us)
Async XLA Ops:
  0.7 0.7 copy-start.1
  22.8 0.7 copy-start.2
  23.5 1.9 %copy-start.4 = (bf16[4096,400]{0,1:T(8,128)(2,1)S(1)}, bf16[4096,400]{0,1:T(8,128)(2,1)}, u32[]{:S(2)}) copy-start(bf16[4096,400]{0,1:T(8,128)(2,1)} %param.8) | copy-start | bytes 9830404
  25.4 16.2 %copy-start.5 = (s32[256,3]{0,1:T(4,128)S(1)}, s32[256,3]{0,1:T(4,128)}, u32[]{:S(2)}) copy-start(s32[256,3]{0,1:T(4,128)} %param.13) | copy-start | bytes 9220
  25.4 16.2 %copy-start.6 = (s32[256]{0:T(256)S(1)}, s32[256]{0:T(256)}, u32[]{:S(2)}) copy-start(s32[256]{0:T(256)} %param.14) | copy-start | bytes 3076
  33.2 23.9 %all-to-all-start.1 = ((bf16[128,8,400]{2,1,0:T(8,128)(2,1)}), bf16[128,8,400]{2,1,0:T(8,128)(2,1)S(1)}, u32[]{:S(2)}, u32[]{:S(2)}) async-start(bf16[128,8,400]{2,1,0:T(8,128)(2,1)} %bitcast.7), calls=%async_computation.1 | async-start | bytes 2097152 | tf_op jit(solution)/shard_map/all_to_all | solution.py:460
  37.4 17.7 %collective-permute-start.2 = (bf16[32,400]{1,0:T(8,128)(2,1)S(1)}, bf16[32,400]{1,0:T(8,128)(2,1)S(1)}, u32[]{:S(2)}, u32[]{:S(2)}) collective-permute-start(bf16[32,400]{1,0:T(8,128)(2,1)S(1)} %get-tuple-element.18.p0), channel_id=1, source_target_pairs={{0,3},{1,0},{2,1},{3,2},{4,7},{5,4},{6,5},{7,6},{8,11},{9,8},{10,9... | collective-permute-start | bytes 76808 | tf_op jit(solution)/shard_map/ppermute | solution.py:47
  40.8 14.4 %collective-permute-start.1 = (bf16[32,400]{1,0:T(8,128)(2,1)S(1)}, bf16[32,400]{1,0:T(8,128)(2,1)S(1)}, u32[]{:S(2)}, u32[]{:S(2)}) collective-permute-start(bf16[32,400]{1,0:T(8,128)(2,1)S(1)} %get-tuple-element.18.p0), channel_id=1, source_target_pairs={{0,2},{1,3},{2,0},{3,1},{4,6},{5,7},{6,4},{7,5},{8,10},{9,11},{10,... | collective-permute-start | bytes 76808 | tf_op jit(solution)/shard_map/ppermute | solution.py:47
  40.9 14.3 %collective-permute-start = (bf16[32,400]{1,0:T(8,128)(2,1)S(1)}, bf16[32,400]{1,0:T(8,128)(2,1)S(1)}, u32[]{:S(2)}, u32[]{:S(2)}) collective-permute-start(bf16[32,400]{1,0:T(8,128)(2,1)S(1)} %get-tuple-element.18.p0), channel_id=1, source_target_pairs={{0,1},{1,2},{2,3},{3,0},{4,5},{5,6},{6,7},{7,4},{8,9},{9,10},{10,1... | collective-permute-start | bytes 76808 | tf_op jit(solution)/shard_map/ppermute | solution.py:47
  57.0 100.0 %copy-start.3 = (s32[32]{0:T(128)S(1)}, s32[32]{0:T(128)}, u32[]{:S(2)}) copy-start(s32[32]{0:T(128)} %param.15) | copy-start | bytes 388
  117.6 1.3 copy-start
  118.9 38.1 %all-to-all-start.2 = ((f32[128,8,400]{2,1,0:T(8,128)}), f32[128,8,400]{2,1,0:T(8,128)S(1)}, u32[]{:S(2)}, u32[]{:S(2)}) async-start(f32[128,8,400]{2,1,0:T(8,128)} %bitcast.22), calls=%async_computation.2 | async-start | bytes 4194304 | tf_op jit(solution)/shard_map/all_to_all | solution.py:464
  126.2 20.6 %collective-permute-start.5 = (f32[32,400]{1,0:T(8,128)S(1)}, f32[32,400]{1,0:T(8,128)S(1)}, u32[]{:S(2)}, u32[]{:S(2)}) collective-permute-start(f32[32,400]{1,0:T(8,128)S(1)} %get-tuple-element.21), channel_id=1, source_target_pairs={{0,1},{1,2},{2,3},{3,0},{4,5},{5,6},{6,7},{7,4},{8,9},{9,10},{10,1... | collective-permute-start | bytes 153608 | tf_op jit(solution)/shard_map/ppermute | solution.py:47
  127.8 26.2 %collective-permute-start.4 = (f32[32,400]{1,0:T(8,128)S(1)}, f32[32,400]{1,0:T(8,128)S(1)}, u32[]{:S(2)}, u32[]{:S(2)}) collective-permute-start(f32[32,400]{1,0:T(8,128)S(1)} %get-tuple-element.22), channel_id=1, source_target_pairs={{0,2},{1,3},{2,0},{3,1},{4,6},{5,7},{6,4},{7,5},{8,10},{9,11},{10,... | collective-permute-start | bytes 153608 | tf_op jit(solution)/shard_map/ppermute | solution.py:47
  130.7 23.3 %collective-permute-start.3 = (f32[32,400]{1,0:T(8,128)S(1)}, f32[32,400]{1,0:T(8,128)S(1)}, u32[]{:S(2)}, u32[]{:S(2)}) collective-permute-start(f32[32,400]{1,0:T(8,128)S(1)} %get-tuple-element.23), channel_id=1, source_target_pairs={{0,3},{1,0},{2,1},{3,2},{4,7},{5,4},{6,5},{7,6},{8,11},{9,8},{10,9... | collective-permute-start | bytes 153608 | tf_op jit(solution)/shard_map/ppermute | solution.py:47
where the time goes:
time: 172 us
  Pallas kernels  97.1 us (56%)
  waiting for transfers between devices  27.3 us (16%)
  starting transfers between devices  21.2 us (12%)
  blocking collectives  21 us (12%)
  local copies, waits for them, and re-layouts  5.29 us (3%)
    pallas_call x1, Pallas kernels, gradients(): pl.pallas_call(grads_kernel, out_shape=(jax.ShapeDtypeStruct((rows, width...  60.5 us
    ppermute x6, waiting for transfers between devices, shifted(): return lax.ppermute(value, axis, pairs)  22.4 us
    all_to_all x1, blocking collectives, local(): asked = exchange(wanted.reshape(devices, 1, lanes)).reshape(devices, lanes)  21 us
    pallas_call x1, Pallas kernels, scatter(): pl.pallas_call(functools.partial(scatter_kernel, slot_count), out_shape=j...  14.9 us
    pallas_call x1, Pallas kernels, relations(): pl.pallas_call(relations_kernel, out_shape=(jax.ShapeDtypeStruct((width,...  13.4 us
    ppermute x6, starting transfers between devices, shifted(): return lax.ppermute(value, axis, pairs)  9.63 us
    pallas_call x1, Pallas kernels, serve(): pl.pallas_call(functools.partial(serve_kernel, slot_count), out_shape=(ja...  7.76 us
    all_to_all x1, starting transfers between devices, local(): exchange(slot_grads.reshape(devices, slot_count, width)).reshape(-1, width)  7.28 us
  transfers between devices with their start and end apart: 8, of which 4 were waited for; matrix products, arithmetic and copies ran while one was open for 0% of the time, Pallas kernels for 8%

commit v1 on v0

--- a/solution.py
+++ b/solution.py
@@ -242,12 +242,12 @@
     inverse = lax.rsqrt(square)
     spread = square * inverse
     above = 1.0 + jnp.exp2(spread - size)
-    slope = (1.0 - slope_weight * pl.reciprocal(above, approx=True)) * (gap * inverse)
+    slope = (1.0 / slope_weight - pl.reciprocal(above, approx=True)) * (gap * inverse)
     return spread, above, slope
 
 
 def grads_kernel(slot_ref, back_ref, shift_ref, size_ref, p0, p1, p2, p3, slots_ref, pool_ref,
-                 entity, spread_out, center, size, grads, slopes, dists, weights, pool_grad):
+                 entity, picks, spread_out, center, size, grads, slopes, dists, weights, pool_grad, codes):
     width, queries = shift_ref.shape
     rows = back_ref.shape[0]
     pool = p0.shape[0]
@@ -269,7 +269,7 @@
 
     spread, above, slope = slope_terms(grads[:, queries:] - center[...], size[...])
     total = jnp.sum(spread + log_weight * jnp.log2(above), axis=0, keepdims=True) * dist_unit
-    weight = (loss_scale * dist_scale) / (1.0 + jnp.exp(margin_gamma - total))
+    weight = (loss_scale * dist_scale * slope_weight) / (1.0 + jnp.exp(margin_gamma - total))
     slope = slope * weight
     grads[:, 0:queries] = -slope
     grads[:, queries:] = slope
@@ -277,76 +277,88 @@
     halves = [pl.ds(half * lanes, lanes) for half in range(queries // lanes)]
     lane = iota((8, lanes), 1)
     group = 4
-    block = 10
+    reach = 50
+
+    def pick(j):
+        source = iota((2 * negatives, near * lanes), 0) & (negatives - 1)
+        target = lax.shift_right_logical(iota(source.shape, 1), 7)
+        return one_hot(source == j * near + target)
+
+    spread_out[0] = dot(entity[...], pick(0), 1, 0)
 
     def chunk(j, _):
         here = j * near
-        picks = iota((2 * negatives, near * lanes), 0) & (negatives - 1)
-        picks = one_hot(picks == here + lax.shift_right_logical(iota(picks.shape, 1), 7))
-        spread_out[...] = dot(entity[...], picks, 1, 0)
+        now = lax.rem(j, 2)
         for first in range(0, near, group):
             def forward(base, count, sums):
                 sums = list(sums)
                 for k in range(group):
                     at = first + k
                     for half, ql in enumerate(halves):
+                        total = sums[half * group + k]
                         product = None
-                        total = sums[half * group + k]
                         for tile in range(count):
                             d = pl.ds(base + tile * 8, 8)
-                            column = spread_out[d, at * lanes : (at + 1) * lanes]
+                            column = spread_out[now, d, at * lanes : (at + 1) * lanes]
                             spread, above, slope = slope_terms(column - center[d, ql], size[d, ql])
                             slopes[at, d, ql] = slope
                             product = above if product is None else product * above
                             total = total + spread
-                        sums[half * group + k] = total + log_weight * jnp.log2(product)
+                            if tile % 4 == 3 or tile == count - 1:
+                                total = total + log_weight * jnp.log2(product)
+                                product = None
+                        sums[half * group + k] = total
                 return tuple(sums)
 
             sums = tuple(jnp.zeros((8, lanes), f32) for _ in range(group * len(halves)))
-            sums = lax.fori_loop(
-                0, tiles // 4, lambda i, s: forward(pl.multiple_of(i * 32, 32), 4, s), sums
-            )
-            if tiles % 4:
-                sums = forward(tiles // 4 * 32, tiles % 4, sums)
+            for start in range(0, tiles, reach):
+                sums = forward(start * 8, min(reach, tiles - start), sums)
             for half, ql in enumerate(halves):
                 for k in range(group):
                     dists[first + k : first + k + 1, ql] = jnp.sum(
                         sums[half * group + k], axis=0, keepdims=True
                     )
-        scale = -loss_scale * dist_scale / negatives
+        scale = -loss_scale * dist_scale * slope_weight / negatives
         weights[...] = scale / (1.0 + jnp.exp(dists[...] * dist_unit - margin_gamma))
         weight_rows = [
             [jnp.broadcast_to(weights[k : k + 1, ql], (8, lanes)) for ql in halves]
             for k in range(near)
         ]
 
-        def backward(i, _):
-            for tile in range(block):
-                d = pl.ds(pl.multiple_of(i * (8 * block), 8) + tile * 8, 8)
-                to_center = [grads[d, ql] for ql in halves]
-                to_pool = pool_grad[d, :]
-                for k in range(near):
-                    row = None
-                    for half, ql in enumerate(halves):
-                        term = slopes[k, d, ql] * weight_rows[k][half]
-                        to_center[half] = to_center[half] - term
-                        row = term if row is None else row + term
-                    row = jnp.sum(row, axis=1, keepdims=True)
-                    to_pool = jnp.where(lane == here + k, row, to_pool)
+        picks[...] = pick(j + 1)
+
+        spread_out[1 - now] = dot(entity[...], picks[...], 1, 0)
+        for tile in range(tiles):
+            d = pl.ds(tile * 8, 8)
+            to_center = [grads[d, ql] for ql in halves]
+            to_pool = pool_grad[d, :]
+            for k in range(near):
+                row = None
                 for half, ql in enumerate(halves):
-                    grads[d, ql] = to_center[half]
-                pool_grad[d, :] = to_pool
-            return 0
-
-        lax.fori_loop(0, tiles // block, backward, 0)
+                    term = slopes[k, d, ql] * weight_rows[k][half]
+                    to_center[half] = to_center[half] - term
+                    row = term if row is None else row + term
+                row = jnp.sum(row, axis=1, keepdims=True)
+                to_pool = jnp.where(lane == here + k, row, to_pool)
+            for half, ql in enumerate(halves):
+                grads[d, ql] = to_center[half]
+            pool_grad[d, :] = to_pool
         return 0
 
     lax.fori_loop(0, negatives // near, chunk, 0)
 
     value = grads[...]
-    high = value.astype(bf16)
-    low = (value - high.astype(f32)).astype(bf16)
-    slots_ref[...] = dot(hot, high, 1, 1) + dot(hot, low, 1, 1)
+    most = jnp.max(jnp.abs(value), axis=0, keepdims=True)
+    power = 14.0 - jnp.floor(jnp.log2(jnp.maximum(most, 1e-30)))
+    level = jnp.minimum(jnp.maximum(jnp.round(value * jnp.exp2(power)), -32767.0), 32767.0)
+    high = jnp.floor(level * (1.0 / 256.0) + 0.5)
+    low = level - high * 256.0
+    codes[...] = jnp.zeros_like(codes)
+    codes[0:width, 0 : 2 * queries] = high.astype(bf16)
+    codes[0:width, 2 * queries :] = low.astype(bf16)
+    codes[width : width + 16, 2 * queries :] = jnp.broadcast_to(power, (16, 2 * queries)).astype(bf16)
+    level = dot(hot, codes[:, 0 : 2 * queries], 1, 1) * 256.0 + dot(hot, codes[:, 2 * queries :], 1, 1)
+    slots_ref[...] = level.astype(i32).astype(jnp.int16)
     pool_ref[...] = jnp.transpose(pool_grad[...])[:, 0:width]
 
 
@@ -360,14 +372,15 @@
     return pl.pallas_call(
         grads_kernel,
         out_shape=(
-            jax.ShapeDtypeStruct((rows, width), f32),
+            jax.ShapeDtypeStruct((rows, padded), jnp.int16),
             jax.ShapeDtypeStruct((negatives, width), f32),
         ),
         in_specs=[whole()] * 8,
         out_specs=(whole(), whole()),
         scratch_shapes=[
             pltpu.VMEM((width, 2 * negatives), bf16),
-            pltpu.VMEM((width, near * lanes), f32),
+            pltpu.VMEM((2 * negatives, near * lanes), bf16),
+            pltpu.VMEM((2, width, near * lanes), f32),
             pltpu.VMEM((width, queries), f32),
             pltpu.VMEM((width, queries), f32),
             pltpu.VMEM((width, 2 * queries), f32),
@@ -375,6 +388,7 @@
             pltpu.VMEM((near, queries), f32),
             pltpu.VMEM((near, queries), f32),
             pltpu.VMEM((padded, negatives), f32),
+            pltpu.VMEM((padded, 4 * queries), bf16),
         ],
         compiler_params=params(48),
         cost_estimate=pl.CostEstimate(
@@ -384,39 +398,37 @@
     )(slot, back, shift, size, *blocks)
 
 
-def scatter_kernel(slot_count, asked_ref, neg_ref, back_ref, own_ref, q1, q2, q3, out_ref, column, both):
+def scatter_kernel(slot_count, asked_ref, neg_ref, back_ref, own_ref, q1, q2, q3, out_ref, column, rows_of, both):
     step = pl.program_id(0)
-    part = out_ref.shape[1]
-    rows, width = back_ref.shape
+    width, part = out_ref.shape
+    rows, padded = back_ref.shape
     pool = q1.shape[0]
 
     @pl.when(step == 0)
     def _():
         column[0:rows, :] = asked_column(asked_ref[...], slot_count)
         here = iota((pool, pool), 0) == iota((pool, pool), 1)
-        column[rows:, :] = jnp.sum(
+        column[rows : rows + pool, :] = jnp.sum(
             jnp.where(here, neg_ref[...].astype(f32), 0.0), axis=1, keepdims=True
         ).astype(i32)
-
-        def place(value, start):
-            size = value.shape[0]
-            high = value.astype(bf16)
-            low = (value - high.astype(f32)).astype(bf16)
-            both[start : start + size, 0:width] = high
-            both[start : start + size, 512 : 512 + width] = low
-
-        both[...] = jnp.zeros_like(both)
-        place(back_ref[...], 0)
-        place(own_ref[...] + q1[...] + q2[...] + q3[...], rows)
-
-    hot = one_hot(iota((rows + pool, part), 1) + step * part == column[...])
-    result = dot(both[...], hot, 0, 0)
-    out_ref[...] = result[0:width, :] + result[512 : 512 + width, :]
+        column[rows + pool :, :] = jnp.full((lanes - pool, 1), -1, i32)
+        level = back_ref[...].astype(i32).astype(f32)
+        rows_of[0:rows, :] = level * jnp.exp2(-level[:, width : width + 1])
+        rows_of[rows:, :] = jnp.zeros((lanes, padded), f32)
+        rows_of[rows : rows + pool, 0:width] = own_ref[...] + q1[...] + q2[...] + q3[...]
+        value = jnp.transpose(rows_of[...])[0:width, :]
+        high = value.astype(bf16)
+        both[0:width, :] = high
+        both[width:, :] = (value - high.astype(f32)).astype(bf16)
+
+    hot = one_hot(iota((rows + lanes, part), 1) + step * part == column[...])
+    result = dot(both[...], hot, 1, 0)
+    out_ref[...] = result[0:width, :] + result[width:, :]
 
 
 def scatter(asked, neg_rows, back, own, others, slot_count, entities):
-    rows, width = back.shape
-    pool = own.shape[0]
+    rows, padded = back.shape
+    pool, width = own.shape
     part = 512
     fixed = lambda i: (0, 0)
     return pl.pallas_call(
@@ -426,11 +438,15 @@
         in_specs=[
             pl.BlockSpec(asked.shape, fixed),
             pl.BlockSpec(neg_rows.shape, fixed),
-            pl.BlockSpec((rows, width), fixed),
+            pl.BlockSpec((rows, padded), fixed),
         ]
         + [pl.BlockSpec((pool, width), fixed)] * 4,
         out_specs=pl.BlockSpec((width, part), lambda i: (0, i)),
-        scratch_shapes=[pltpu.VMEM((rows + pool, 1), i32), pltpu.VMEM((rows + pool, 1024), bf16)],
+        scratch_shapes=[
+            pltpu.VMEM((rows + lanes, 1), i32),
+            pltpu.VMEM((rows + lanes, padded), f32),
+            pltpu.VMEM((2 * width, rows + lanes), bf16),
+        ],
         compiler_params=params(48),
         name="scatter",
     )(asked, neg_rows, back, own, *others)
@@ -461,7 +477,8 @@
     shift, size = relations(rel_ids.T, query_type.reshape(1, queries), rel_center.T, rel_offset.T)
     blocks = [block] + [shifted(block, "blk", step) for step in range(1, group_size)]
     slot_grads, pool_grads = gradients(slot, back, shift, size, blocks)
-    returned = exchange(slot_grads.reshape(devices, slot_count, width)).reshape(-1, width)
+    padded = slot_grads.shape[1]
+    returned = exchange(slot_grads.reshape(devices, slot_count, padded)).reshape(-1, padded)
     others = [
         shifted(pool_grads[step * pool : (step + 1) * pool], "blk", -step)
         for step in range(1, group_size)

time: 172 us -> 137 us (0.80)
  Pallas kernels: 97.1 us -> 74.8 us
  waiting for transfers between devices: 27.3 us -> 15.9 us
    pallas_call x1, Pallas kernels: 60.5 us -> 40.6 us  [gradients(): pl.pallas_call(grads_kernel, out_shape=(jax.ShapeDtypeStruct((rows, padde...]
    ppermute x6, waiting for transfers between devices: 22.4 us -> 12.7 us  [shifted(): return lax.ppermute(value, axis, pairs)]
    pallas_call x1, Pallas kernels: 14.9 us -> 12.5 us  [scatter(): pl.pallas_call(functools.partial(scatter_kernel, slot_count), out_shape=j...]
    all_to_all x1, waiting for transfers between devices: 3.03 us -> 1.24 us  [local(): exchange(slot_grads.reshape(devices, slot_count, padded))]
    unnamed x15 -> x13, local copies, waits for them, and re-layouts: 5.27 us -> 3.96 us
  transfers between devices with their start and end apart: 8 -> 8, of which waited for: 4 -> 4; matrix products, arithmetic and copies ran while one was open for 0% -> 0% of each run, Pallas kernels for 8% -> 10%
where the time goes in v1:
time: 137 us
  Pallas kernels  74.8 us (55%)
  starting transfers between devices  21.4 us (16%)
  blocking collectives  21 us (15%)
  waiting for transfers between devices  15.9 us (12%)
  local copies, waits for them, and re-layouts  3.98 us (3%)
    pallas_call x1, Pallas kernels, gradients(): pl.pallas_call(grads_kernel, out_shape=(jax.ShapeDtypeStruct((rows, padde...  40.6 us
    all_to_all x1, blocking collectives, local(): asked = exchange(wanted.reshape(devices, 1, lanes)).reshape(devices, lanes)  21 us
    pallas_call x1, Pallas kernels, relations(): pl.pallas_call(relations_kernel, out_shape=(jax.ShapeDtypeStruct((width,...  13.4 us
    ppermute x6, waiting for transfers between devices, shifted(): return lax.ppermute(value, axis, pairs)  12.7 us
    pallas_call x1, Pallas kernels, scatter(): pl.pallas_call(functools.partial(scatter_kernel, slot_count), out_shape=j...  12.5 us
    ppermute x6, starting transfers between devices, shifted(): return lax.ppermute(value, axis, pairs)  9.81 us
    pallas_call x1, Pallas kernels, serve(): pl.pallas_call(functools.partial(serve_kernel, slot_count), out_shape=(ja...  7.75 us
    all_to_all x1, starting transfers between devices, local(): exchange(slot_grads.reshape(devices, slot_count, padded))  7.28 us
  transfers between devices with their start and end apart: 8, of which 4 were waited for; matrix products, arithmetic and copies ran while one was open for 0% of the time, Pallas kernels for 10%

profile of v1, /device:TPU:1, one launch (start us, length us, event | category | flops | bytes accessed | tf_op | source)
XLA Modules:
  0.0 137.0 jit_solution(8276811097275038292)
XLA Ops:
  0.0 0.7 copy.12
  0.7 0.0 copy-start
  0.7 0.7 copy-done
  1.4 0.5 plan_slots.1
  1.8 21.0 %all_to_all.15 = s32[128,1,128]{2,1,0:T(1,128)S(1)} all-to-all(s32[128,1,128]{2,1,0:T(1,128)S(1)} %bitcast.25), channel_id=1, replica_groups=mesh['table'=32,'blk'=4] {'table','blk'}, dimensions={0} | all-to-all | bytes 131072 | tf_op jit(solution)/shard_map/all_to_all | solution.py:474
  22.8 0.0 copy-start.1
  22.8 0.7 copy-done.1
  23.5 0.0 copy-start.3
  23.5 1.9 %copy-done.3 = bf16[4096,400]{0,1:T(8,128)(2,1)S(1)} copy-done((bf16[4096,400]{0,1:T(8,128)(2,1)S(1)}, bf16[4096,400]{0,1:T(8,128)(2,1)}, u32[]{:S(2)}) %copy-start.3) | copy-done | bytes 3276824
  25.4 7.8 %serve.1 = (bf16[1024,400]{1,0:T(8,128)(2,1)}, bf16[32,400]{1,0:T(8,128)(2,1)S(1)}) custom-call(s32[128,128]{1,0:T(8,128)S(1)} %bitcast.23, s32[1,32]{1,0:T(1,128)S(1)} %bitcast.28, bf16[400,4096]{1,0:T(8,128)(2,1)S(1)} %bitcast.30), custom_call_target="tpu_custom_call" | custom-call | flops 3460300800 | bytes 3276800 | tf_op jit(solution)/shard_map/serve/pallas_call | solution.py:135
  33.2 4.3 %all-to-all-start.1 = ((bf16[128,8,400]{2,1,0:T(8,128)(2,1)}), bf16[128,8,400]{2,1,0:T(8,128)(2,1)S(1)}, u32[]{:S(2)}, u32[]{:S(2)}) async-start(bf16[128,8,400]{2,1,0:T(8,128)(2,1)} %bitcast.7), calls=%async_computation.1 | async-start | bytes 2097152 | tf_op jit(solution)/shard_map/all_to_all | solution.py:476
  37.4 3.3 %collective-permute-start.2 = (bf16[32,400]{1,0:T(8,128)(2,1)S(1)}, bf16[32,400]{1,0:T(8,128)(2,1)S(1)}, u32[]{:S(2)}, u32[]{:S(2)}) collective-permute-start(bf16[32,400]{1,0:T(8,128)(2,1)S(1)} %get-tuple-element.18.p0), channel_id=1, source_target_pairs={{0,3},{1,0},{2,1},{3,2},{4,7},{5,4},{6,5},{7,6},{8,11},{9,8},{10,9... | collective-permute-start | bytes 76808 | tf_op jit(solution)/shard_map/ppermute | solution.py:47
  40.8 0.1 collective-permute-start.1
  40.9 0.8 collective-permute-start
  41.7 0.0 copy-done.4
  41.7 0.0 copy-done.5
  41.7 13.4 %relations.1 = (f32[400,256]{1,0:T(8,128)S(1)}, f32[400,256]{1,0:T(8,128)S(1)}) custom-call(s32[3,256]{1,0:T(4,128)S(1)} %bitcast.31, s32[1,256]{1,0:T(1,128)S(1)} %bitcast.32, bf16[400,7424]{1,0:T(8,128)(2,1)} %bitcast.33, bf16[400,7424]{1,0:T(8,128)(2,1)} %bitcast.34), custom_call_target="tpu_custom_call" | custom-call | flops 6081740800 | bytes 11878400 | tf_op jit(solution)/shard_map/relations/pallas_call | solution.py:214
  55.1 0.0 collective-permute-done.2.p3
  55.1 0.0 collective-permute-done.1.p2
  55.1 0.0 collective-permute-done.p1
  55.1 1.9 %all-to-all-done.1 = bf16[128,8,400]{2,1,0:T(8,128)(2,1)S(1)} async-done(((bf16[128,8,400]{2,1,0:T(8,128)(2,1)}), bf16[128,8,400]{2,1,0:T(8,128)(2,1)S(1)}, u32[]{:S(2)}, u32[]{:S(2)}) %all-to-all-start.1) | async-done | bytes 819232 | tf_op jit(solution)/shard_map/all_to_all | solution.py:476
  57.0 40.6 %gradients.1 = (s16[1024,512]{1,0:T(8,128)(2,1)}, f32[128,400]{1,0:T(8,128)S(1)}) custom-call(s32[1,512]{1,0:T(1,128)S(1)} %get-tuple-element.14.slot_ref, bf16[1024,400]{1,0:T(8,128)(2,1)S(1)} %bitcast.22, f32[400,256]{1,0:T(8,128)S(1)} %get-tuple-element.16.shift_ref, f32[400,256]{1,0:T(8,128)S(1)} %get-tuple-element.17.size_ref, ...), custom_call_target="tpu_custom_call" | custom-call | flops 209715200 | bytes 1638400 | tf_op jit(solution)/shard_map/gradients/pallas_call | solution.py:372
  97.6 7.3 %all-to-all-start.2 = ((s16[128,8,512]{2,1,0:T(8,128)(2,1)}), s16[128,8,512]{2,1,0:T(8,128)(2,1)S(1)}, u32[]{:S(2)}, u32[]{:S(2)}) async-start(s16[128,8,512]{2,1,0:T(8,128)(2,1)} %bitcast.13), calls=%async_computation.2 | async-start | bytes 2097152 | tf_op jit(solution)/shard_map/all_to_all | solution.py:481
  104.9 1.8 %collective-permute-start.5 = (f32[32,400]{1,0:T(8,128)S(1)}, f32[32,400]{1,0:T(8,128)S(1)}, u32[]{:S(2)}, u32[]{:S(2)}) collective-permute-start(f32[32,400]{1,0:T(8,128)S(1)} %get-tuple-element.21), channel_id=1, source_target_pairs={{0,1},{1,2},{2,3},{3,0},{4,5},{5,6},{6,7},{7,4},{8,9},{9,10},{10,1... | collective-permute-start | bytes 153608 | tf_op jit(solution)/shard_map/ppermute | solution.py:47
  106.7 2.9 %collective-permute-start.4 = (f32[32,400]{1,0:T(8,128)S(1)}, f32[32,400]{1,0:T(8,128)S(1)}, u32[]{:S(2)}, u32[]{:S(2)}) collective-permute-start(f32[32,400]{1,0:T(8,128)S(1)} %get-tuple-element.22), channel_id=1, source_target_pairs={{0,2},{1,3},{2,0},{3,1},{4,6},{5,7},{6,4},{7,5},{8,10},{9,11},{10,... | collective-permute-start | bytes 153608 | tf_op jit(solution)/shard_map/ppermute | solution.py:47
  109.6 0.9 collective-permute-start.3
  110.6 8.0 %collective-permute-done.5.q3 = f32[32,400]{1,0:T(8,128)S(1)} collective-permute-done((f32[32,400]{1,0:T(8,128)S(1)}, f32[32,400]{1,0:T(8,128)S(1)}, u32[]{:S(2)}, u32[]{:S(2)}) %collective-permute-start.5) | collective-permute-done | bytes 51232 | tf_op jit(solution)/shard_map/ppermute | solution.py:47
  118.5 4.7 %collective-permute-done.4.q2 = f32[32,400]{1,0:T(8,128)S(1)} collective-permute-done((f32[32,400]{1,0:T(8,128)S(1)}, f32[32,400]{1,0:T(8,128)S(1)}, u32[]{:S(2)}, u32[]{:S(2)}) %collective-permute-start.4) | collective-permute-done | bytes 51232 | tf_op jit(solution)/shard_map/ppermute | solution.py:47
  123.3 0.0 collective-permute-done.3.q1
  123.3 1.2 all-to-all-done.2
  124.5 0.0 copy-done.2
  124.5 12.5 %scatter.1 = f32[400,4096]{1,0:T(8,128)} custom-call(s32[128,128]{1,0:T(8,128)S(1)} %bitcast.24, s32[1,32]{1,0:T(1,128)S(1)} %bitcast.29, s16[1024,512]{1,0:T(8,128)(2,1)S(1)} %bitcast.21, f32[32,400]{1,0:T(8,128)S(1)} %get-tuple-element.24.own_ref, f32[32,400]{1,0:T(8,128)S(1)} %collective-permute-done.3.q1, f32[32,400]{1,0:T(8,128)S(1)} %collective-permute-done.4.q2, ...), custom_call_target="tpu_custom_call" | custom-call | tf_op jit(solution)/shard_map/scatter/pallas_call | solution.py:434
  (4 shorter events, 0.0 us)
Async XLA Ops:
  0.7 0.7 copy-start
  22.8 0.7 copy-start.1
  23.5 1.9 %copy-start.3 = (bf16[4096,400]{0,1:T(8,128)(2,1)S(1)}, bf16[4096,400]{0,1:T(8,128)(2,1)}, u32[]{:S(2)}) copy-start(bf16[4096,400]{0,1:T(8,128)(2,1)} %param.8) | copy-start | bytes 9830404
  25.4 16.2 %copy-start.4 = (s32[256,3]{0,1:T(4,128)S(1)}, s32[256,3]{0,1:T(4,128)}, u32[]{:S(2)}) copy-start(s32[256,3]{0,1:T(4,128)} %param.13) | copy-start | bytes 9220
  25.4 16.2 %copy-start.5 = (s32[256]{0:T(256)S(1)}, s32[256]{0:T(256)}, u32[]{:S(2)}) copy-start(s32[256]{0:T(256)} %param.14) | copy-start | bytes 3076
  33.2 23.9 %all-to-all-start.1 = ((bf16[128,8,400]{2,1,0:T(8,128)(2,1)}), bf16[128,8,400]{2,1,0:T(8,128)(2,1)S(1)}, u32[]{:S(2)}, u32[]{:S(2)}) async-start(bf16[128,8,400]{2,1,0:T(8,128)(2,1)} %bitcast.7), calls=%async_computation.1 | async-start | bytes 2097152 | tf_op jit(solution)/shard_map/all_to_all | solution.py:476
  37.4 17.7 %collective-permute-start.2 = (bf16[32,400]{1,0:T(8,128)(2,1)S(1)}, bf16[32,400]{1,0:T(8,128)(2,1)S(1)}, u32[]{:S(2)}, u32[]{:S(2)}) collective-permute-start(bf16[32,400]{1,0:T(8,128)(2,1)S(1)} %get-tuple-element.18.p0), channel_id=1, source_target_pairs={{0,3},{1,0},{2,1},{3,2},{4,7},{5,4},{6,5},{7,6},{8,11},{9,8},{10,9... | collective-permute-start | bytes 76808 | tf_op jit(solution)/shard_map/ppermute | solution.py:47
  40.8 14.4 %collective-permute-start.1 = (bf16[32,400]{1,0:T(8,128)(2,1)S(1)}, bf16[32,400]{1,0:T(8,128)(2,1)S(1)}, u32[]{:S(2)}, u32[]{:S(2)}) collective-permute-start(bf16[32,400]{1,0:T(8,128)(2,1)S(1)} %get-tuple-element.18.p0), channel_id=1, source_target_pairs={{0,2},{1,3},{2,0},{3,1},{4,6},{5,7},{6,4},{7,5},{8,10},{9,11},{10,... | collective-permute-start | bytes 76808 | tf_op jit(solution)/shard_map/ppermute | solution.py:47
  40.9 14.3 %collective-permute-start = (bf16[32,400]{1,0:T(8,128)(2,1)S(1)}, bf16[32,400]{1,0:T(8,128)(2,1)S(1)}, u32[]{:S(2)}, u32[]{:S(2)}) collective-permute-start(bf16[32,400]{1,0:T(8,128)(2,1)S(1)} %get-tuple-element.18.p0), channel_id=1, source_target_pairs={{0,1},{1,2},{2,3},{3,0},{4,5},{5,6},{6,7},{7,4},{8,9},{9,10},{10,1... | collective-permute-start | bytes 76808 | tf_op jit(solution)/shard_map/ppermute | solution.py:47
  57.0 67.5 %copy-start.2 = (s32[32]{0:T(128)S(1)}, s32[32]{0:T(128)}, u32[]{:S(2)}) copy-start(s32[32]{0:T(128)} %param.15) | copy-start | bytes 388
  97.6 26.9 %all-to-all-start.2 = ((s16[128,8,512]{2,1,0:T(8,128)(2,1)}), s16[128,8,512]{2,1,0:T(8,128)(2,1)S(1)}, u32[]{:S(2)}, u32[]{:S(2)}) async-start(s16[128,8,512]{2,1,0:T(8,128)(2,1)} %bitcast.13), calls=%async_computation.2 | async-start | bytes 2097152 | tf_op jit(solution)/shard_map/all_to_all | solution.py:481
  104.9 13.6 %collective-permute-start.5 = (f32[32,400]{1,0:T(8,128)S(1)}, f32[32,400]{1,0:T(8,128)S(1)}, u32[]{:S(2)}, u32[]{:S(2)}) collective-permute-start(f32[32,400]{1,0:T(8,128)S(1)} %get-tuple-element.21), channel_id=1, source_target_pairs={{0,1},{1,2},{2,3},{3,0},{4,5},{5,6},{6,7},{7,4},{8,9},{9,10},{10,1... | collective-permute-start | bytes 153608 | tf_op jit(solution)/shard_map/ppermute | solution.py:47
  106.7 16.6 %collective-permute-start.4 = (f32[32,400]{1,0:T(8,128)S(1)}, f32[32,400]{1,0:T(8,128)S(1)}, u32[]{:S(2)}, u32[]{:S(2)}) collective-permute-start(f32[32,400]{1,0:T(8,128)S(1)} %get-tuple-element.22), channel_id=1, source_target_pairs={{0,2},{1,3},{2,0},{3,1},{4,6},{5,7},{6,4},{7,5},{8,10},{9,11},{10,... | collective-permute-start | bytes 153608 | tf_op jit(solution)/shard_map/ppermute | solution.py:47
  109.6 13.6 %collective-permute-start.3 = (f32[32,400]{1,0:T(8,128)S(1)}, f32[32,400]{1,0:T(8,128)S(1)}, u32[]{:S(2)}, u32[]{:S(2)}) collective-permute-start(f32[32,400]{1,0:T(8,128)S(1)} %get-tuple-element.23), channel_id=1, source_target_pairs={{0,3},{1,0},{2,1},{3,2},{4,7},{5,4},{6,5},{7,6},{8,11},{9,8},{10,9... | collective-permute-start | bytes 153608 | tf_op jit(solution)/shard_map/ppermute | solution.py:47

commit v2 on v1

--- a/solution.py
+++ b/solution.py
@@ -22,6 +22,7 @@
 log_weight = (1.0 - inside_weight) / inside_weight
 slope_weight = 1.0 - inside_weight
 lanes = 128
+MESH = pl.DeviceIdType.MESH
 near = 8
 
 
@@ -51,134 +52,132 @@
     return jnp.where(mask, 1.0, 0.0).astype(bf16)
 
 
-def slots_kernel(slot_count, devices, owner_ref, row_ref, wanted_ref, slot_ref):
+def plan_slots(owner_ref, row_ref, slot_count, devices, mates):
     owner = jnp.concatenate([owner_ref[0:1, :], owner_ref[1:2, :]], axis=1)
     row = jnp.concatenate([row_ref[0:1, :], row_ref[1:2, :]], axis=1)
     requests = owner.shape[1]
-    named = iota((devices, requests), 0) == owner
+    bits = int(math.log2(mates))
+    place = (owner & (mates - 1)) * (devices // mates) + lax.shift_right_logical(owner, bits)
+    named = iota((devices, requests), 0) == place
     named_hot = one_hot(named)
     earlier = one_hot(iota((requests, requests), 0) < iota((requests, requests), 1))
     before = dot(named_hot, earlier, 1, 0)
     rank = jnp.sum(jnp.where(named, before, 0.0), axis=0, keepdims=True).astype(i32)
-    slot_ref[...] = owner * slot_count + rank
     high = lax.shift_right_logical(row, 6)
     low = row - high * 64
-    ranked = iota((lanes, requests), 0) == rank
-    high_hot = jnp.where(ranked, high.astype(f32), 0.0).astype(bf16)
-    low_hot = jnp.where(ranked, low.astype(f32), 0.0).astype(bf16)
-    asked = dot(named_hot, high_hot, 1, 1) * 64.0 + dot(named_hot, low_hot, 1, 1)
-    wanted_ref[...] = asked.astype(i32)
-
-
-def plan_slots(owner, row, slot_count, devices):
-    requests = owner.shape[0] * owner.shape[1]
-    return pl.pallas_call(
-        functools.partial(slots_kernel, slot_count, devices),
-        out_shape=(
-            jax.ShapeDtypeStruct((devices, lanes), i32),
-            jax.ShapeDtypeStruct((1, requests), i32),
-        ),
-        in_specs=[whole(), whole()],
-        out_specs=(whole(), whole()),
-        compiler_params=params(32),
-        name="plan_slots",
-    )(owner, row)
+    lane = iota((lanes, requests), 0)
+    parts = jnp.where(lane == rank, high.astype(f32), 0.0)
+    parts = parts + jnp.where(lane == rank + slot_count, low.astype(f32), 0.0)
+    return owner * slot_count + rank, dot(named_hot, parts.astype(bf16), 1, 1)
 
 
 def asked_column(asked, slot_count):
     devices = asked.shape[0]
     rows = devices * slot_count
-    high = lax.shift_right_logical(asked, 6)
-    low = asked - high * 64
     group = lax.shift_right_logical(iota((rows, devices), 0), int(math.log2(slot_count)))
     pick = one_hot(group == iota((rows, devices), 1))
-    spread = dot(pick, high.astype(f32).astype(bf16), 1, 0) * 64.0 + dot(
-        pick, low.astype(f32).astype(bf16), 1, 0
-    )
-    mine = (iota((rows, lanes), 0) & (slot_count - 1)) == iota((rows, lanes), 1)
-    return jnp.sum(jnp.where(mine, spread, 0.0), axis=1, keepdims=True).astype(i32)
-
-
-def serve_kernel(slot_count, asked_ref, neg_ref, table_ref, served_ref, pool_ref, total, column):
-    step = pl.program_id(0)
-    part = table_ref.shape[1]
-    rows = served_ref.shape[0]
-    pool = pool_ref.shape[0]
-
-    @pl.when(step == 0)
-    def _():
-        column[0:rows, :] = asked_column(asked_ref[...], slot_count)
-        here = iota((pool, pool), 0) == iota((pool, pool), 1)
-        column[rows : rows + pool, :] = jnp.sum(
-            jnp.where(here, neg_ref[...].astype(f32), 0.0), axis=1, keepdims=True
-        ).astype(i32)
-        total[...] = jnp.zeros_like(total)
-
-    base = step * part
-    for start in range(0, rows + pool, 256):
-        size = min(256, rows + pool - start)
-        block = pl.ds(start, size)
-        hot = one_hot(iota((size, part), 1) + base == column[block, :])
-        total[block, :] += dot(hot, table_ref[...], 1, 1)
-
-    @pl.when(step == pl.num_programs(0) - 1)
-    def _():
-        served_ref[...] = total[0:rows, :].astype(bf16)
-        pool_ref[...] = total[rows : rows + pool, :].astype(bf16)
-
-
-def serve(asked, neg_rows, table, slot_count):
-    width, entities = table.shape
-    rows = asked.shape[0] * slot_count
-    pool = neg_rows.shape[1]
-    part = 1024
-    return pl.pallas_call(
-        functools.partial(serve_kernel, slot_count),
-        out_shape=(
-            jax.ShapeDtypeStruct((rows, width), bf16),
-            jax.ShapeDtypeStruct((pool, width), bf16),
-        ),
-        grid=(entities // part,),
-        in_specs=[
-            pl.BlockSpec(asked.shape, lambda i: (0, 0)),
-            pl.BlockSpec(neg_rows.shape, lambda i: (0, 0)),
-            pl.BlockSpec((width, part), lambda i: (0, i)),
-        ],
-        out_specs=(
-            pl.BlockSpec((rows, width), lambda i: (0, 0)),
-            pl.BlockSpec((pool, width), lambda i: (0, 0)),
-        ),
-        scratch_shapes=[pltpu.VMEM((rows + pool, width), f32), pltpu.VMEM((rows + pool, 1), i32)],
-        compiler_params=params(40),
-        cost_estimate=pl.CostEstimate(
-            flops=2 * (rows + pool) * width * entities,
-            bytes_accessed=2 * width * entities,
-            transcendentals=0,
-        ),
-        name="serve",
-    )(asked, neg_rows, table)
+    spread = dot(pick, asked.astype(bf16), 1, 0)
+    slot = iota((rows, lanes), 0) & (slot_count - 1)
+    lane = iota((rows, lanes), 1)
+    row = jnp.where(lane == slot, spread * 64.0, jnp.where(lane == slot + slot_count, spread, 0.0))
+    return jnp.sum(row, axis=1, keepdims=True).astype(i32)
+
+
+def column_of(row):
+    size = row.shape[1]
+    here = iota((size, size), 0) == iota((size, size), 1)
+    return jnp.sum(jnp.where(here, row.astype(f32), 0.0), axis=1, keepdims=True).astype(i32)
 
 
 def softplus(x):
     return jnp.maximum(x, 0.0) + jnp.log1p(jnp.exp(-jnp.abs(x)))
 
 
-def relations_kernel(ids_ref, type_ref, center_hbm, offset_hbm, shift_ref, size_ref,
-                     center_tab, offset_tab, center_sum, offset_rows, sems):
+def fetch_kernel(
+    slot_count, table_size, group_size,
+    owner_ref, row_ref, neg_ref, ids_ref, type_ref, table_hbm, center_hbm, offset_hbm,
+    slot_ref, asked_ref, back_ref, block_ref, shift_ref, size_ref,
+    table, center_tab, offset_tab, center_sum, offset_rows, wanted, passed, ordered, served, column,
+    load_sems, first_send, first_recv, second_send, second_recv, row_send, row_recv,
+    pool_send, pool_recv,
+):
     hops, queries = ids_ref.shape
     width, rels = center_tab.shape
-    copies = [
-        pltpu.make_async_copy(center_hbm, center_tab, sems.at[0]),
-        pltpu.make_async_copy(offset_hbm, offset_tab, sems.at[1]),
+    entities = table.shape[1]
+    devices = table_size * group_size
+    mates = 2 * group_size
+    teams = devices // mates
+    row_me, col_me = lax.axis_index("table"), lax.axis_index("blk")
+    me = row_me * group_size + col_me
+    mate, team = lax.rem(me, mates), lax.div(me, mates)
+
+    def target(index):
+        return (lax.div(index, group_size), lax.rem(index, group_size))
+
+    loads = [
+        pltpu.make_async_copy(source, place, load_sems.at[i])
+        for i, (source, place) in enumerate(
+            [(table_hbm, table), (center_hbm, center_tab), (offset_hbm, offset_tab)]
+        )
     ]
-    for copy in copies:
-        copy.start()
+    for load in loads:
+        load.start()
+
+    barrier = pltpu.get_barrier_semaphore()
+
+    def greet(i, _):
+        pl.semaphore_signal(
+            barrier, inc=1, device_id=target(lax.rem(me + i, devices)), device_id_type=MESH
+        )
+        return 0
+
+    lax.fori_loop(1, devices, greet, 0)
+
+    slot, asked = plan_slots(owner_ref, row_ref, slot_count, devices, mates)
+    slot_ref[...] = slot
+    wanted[...] = asked.reshape(mates, teams, lanes)
     center_sum[...] = jnp.zeros_like(center_sum)
     offset_rows[...] = jnp.zeros_like(offset_rows)
-    for copy in copies:
-        copy.wait()
-
-    def part(base, size):
+
+    pl.semaphore_wait(barrier, devices - 1)
+
+    def first_hop(i, _):
+        other = lax.rem(mate + i, mates)
+        pltpu.make_async_remote_copy(
+            src_ref=wanted.at[other], dst_ref=passed.at[mate],
+            send_sem=first_send, recv_sem=first_recv,
+            device_id=target(team * mates + other), device_id_type=MESH,
+        ).start()
+        return 0
+
+    lax.fori_loop(1, mates, first_hop, 0)
+
+    loads[0].wait()
+
+    def rows_at(rows):
+        total = None
+        for start in range(0, entities, 1024):
+            hot = one_hot(iota((rows.shape[0], 1024), 1) + start == rows)
+            part = dot(hot, table[:, start : start + 1024], 1, 1)
+            total = part if total is None else total + part
+        return total.astype(bf16)
+
+    block_ref[0] = rows_at(column_of(neg_ref[...]))
+    pool_copies = []
+    for step in range(1, group_size):
+        copy = pltpu.make_async_remote_copy(
+            src_ref=block_ref.at[0], dst_ref=block_ref.at[step],
+            send_sem=pool_send.at[step], recv_sem=pool_recv.at[step],
+            device_id=(row_me, lax.rem(col_me + step, group_size)), device_id_type=MESH,
+        )
+        copy.start()
+        pool_copies.append(copy)
+
+    def await_all(ref, count, sem):
+        part = ref.at[pl.ds(0, count)]
+        pltpu.make_async_copy(part, part, sem).wait()
+
+    def relations(base, size):
         columns = pl.ds(base, size)
         count = jnp.zeros((size, queries), f32)
         hots = []
@@ -192,49 +191,121 @@
             offset_rows[:, here] += dot(offset_tab[:, columns], hots[hop], 1, 0)
 
     step = 1024
-
-    def body(i, _):
-        part(pl.multiple_of(i * step, step), step)
+    whole_steps = rels // step
+    cuts = (0, 2, 4, whole_steps)
+
+    def relations_part(i):
+        def body(k, _):
+            relations(pl.multiple_of(k * step, step), step)
+            return 0
+
+        lax.fori_loop(cuts[i], cuts[i + 1], body, 0)
+
+    passed[mate] = wanted[mate]
+    await_all(wanted, mates - 1, first_send)
+    await_all(passed, mates - 1, first_recv)
+    source, target_row = iota((devices, devices), 1), iota((devices, devices), 0)
+    mate_bits, team_bits = int(math.log2(mates)), int(math.log2(teams))
+    order = one_hot(
+        (target_row & (mates - 1)) * teams + lax.shift_right_logical(target_row, mate_bits) == source
+    )
+    ordered[...] = dot(order, passed[...].reshape(devices, lanes).astype(bf16), 1, 0).reshape(
+        teams, mates, lanes
+    )
+
+    def second_hop(i, _):
+        other = lax.rem(team + i, teams)
+        pltpu.make_async_remote_copy(
+            src_ref=ordered.at[other], dst_ref=asked_ref.at[team],
+            send_sem=second_send, recv_sem=second_recv,
+            device_id=target(other * mates + mate), device_id_type=MESH,
+        ).start()
         return 0
 
-    lax.fori_loop(0, rels // step, body, 0)
+    lax.fori_loop(1, teams, second_hop, 0)
+    loads[1].wait()
+    loads[2].wait()
+    relations_part(0)
+    asked_ref[team] = ordered[team]
+    await_all(ordered, teams - 1, second_send)
+    await_all(asked_ref, teams - 1, second_recv)
+
+    column[...] = asked_column(asked_ref[...].reshape(devices, lanes), slot_count)
+    quarter = devices // 4
+    mine, inside = lax.div(me, quarter), lax.rem(me, quarter)
+    for turn in (1, 2, 3, 0):
+        part = lax.rem(mine + turn, 4)
+        size = quarter * slot_count
+        rows = rows_at(column[pl.ds(pl.multiple_of(part * size, size), size), :])
+        served[pl.ds(part * quarter, quarter)] = rows.reshape(quarter, slot_count, width)
+
+        def send_rows(i, _):
+            other = part * quarter + lax.rem(inside + i, quarter)
+            pltpu.make_async_remote_copy(
+                src_ref=served.at[other], dst_ref=back_ref.at[me],
+                send_sem=row_send, recv_sem=row_recv,
+                device_id=target(other), device_id_type=MESH,
+            ).start()
+            return 0
+
+        lax.fori_loop(1 if turn == 0 else 0, quarter, send_rows, 0)
+
+    back_ref[me] = served[me]
+    relations_part(1)
+    relations_part(2)
     if rels % step:
-        part(rels // step * step, rels % step)
+        relations(whole_steps * step, rels % step)
     shift_ref[...] = center_sum[...]
     total = jnp.zeros((width, queries), f32)
     for hop in range(hops):
         value = softplus(offset_rows[:, hop * queries : (hop + 1) * queries])
         total = total + jnp.where(type_ref[...] >= hop, value, 0.0)
     size_ref[...] = total
-
-
-def relations(rel_ids, query_type, rel_center, rel_offset):
+    for copy in pool_copies:
+        copy.wait()
+    await_all(served, devices - 1, row_send)
+    await_all(back_ref, devices - 1, row_recv)
+
+
+def fetch(owner, row, neg_row, rel_ids, query_type, table, rel_center, rel_offset, slot_count,
+          table_size, group_size):
     hops, queries = rel_ids.shape
     width, rels = rel_center.shape
+    entities = table.shape[1]
+    devices = table_size * group_size
+    mates = 2 * group_size
+    teams = devices // mates
+    pool = neg_row.shape[1]
+    anywhere = pl.BlockSpec(memory_space=pl.ANY)
+    dma = pltpu.SemaphoreType.DMA
     return pl.pallas_call(
-        relations_kernel,
+        functools.partial(fetch_kernel, slot_count, table_size, group_size),
         out_shape=(
+            jax.ShapeDtypeStruct((1, 2 * queries), i32),
+            jax.ShapeDtypeStruct((teams, mates, lanes), f32),
+            jax.ShapeDtypeStruct((devices, slot_count, width), bf16),
+            jax.ShapeDtypeStruct((group_size, pool, width), bf16),
             jax.ShapeDtypeStruct((width, queries), f32),
             jax.ShapeDtypeStruct((width, queries), f32),
         ),
-        in_specs=[whole(), whole(), pl.BlockSpec(memory_space=pl.ANY),
-                  pl.BlockSpec(memory_space=pl.ANY)],
-        out_specs=(whole(), whole()),
+        in_specs=[whole()] * 5 + [anywhere] * 3,
+        out_specs=(whole(),) * 6,
         scratch_shapes=[
+            pltpu.VMEM((width, entities), bf16),
             pltpu.VMEM((width, rels), bf16),
             pltpu.VMEM((width, rels), bf16),
             pltpu.VMEM((width, queries), f32),
             pltpu.VMEM((width, hops * queries), f32),
-            pltpu.SemaphoreType.DMA((2,)),
+            pltpu.VMEM((mates, teams, lanes), f32),
+            pltpu.VMEM((mates, teams, lanes), f32),
+            pltpu.VMEM((teams, mates, lanes), f32),
+            pltpu.VMEM((devices, slot_count, width), bf16),
+            pltpu.VMEM((devices * slot_count, 1), i32),
+            dma((3,)), dma, dma, dma, dma, dma, dma, dma((group_size,)), dma((group_size,)),
         ],
-        compiler_params=params(48),
-        cost_estimate=pl.CostEstimate(
-            flops=2 * (hops + 1) * queries * width * rels,
-            bytes_accessed=4 * width * rels,
-            transcendentals=0,
-        ),
-        name="relations",
-    )(rel_ids, query_type, rel_center, rel_offset)
+        compiler_params=params(52, collective_id=0, has_side_effects=True),
+        name="fetch",
+    )(owner, row, neg_row, rel_ids, query_type, table, rel_center, rel_offset)
 
 
 def slope_terms(gap, size):
@@ -246,12 +317,11 @@
     return spread, above, slope
 
 
-def grads_kernel(slot_ref, back_ref, shift_ref, size_ref, p0, p1, p2, p3, slots_ref, pool_ref,
+def grads_kernel(slot_ref, back_ref, shift_ref, size_ref, block_ref, slots_ref, pool_ref,
                  entity, picks, spread_out, center, size, grads, slopes, dists, weights, pool_grad, codes):
     width, queries = shift_ref.shape
     rows = back_ref.shape[0]
-    pool = p0.shape[0]
-    negatives = 4 * pool
+    negatives = block_ref.shape[0]
     tiles = width // 8
 
     hot = one_hot(iota((rows, 2 * queries), 0) == slot_ref[...])
@@ -259,9 +329,8 @@
     center[...] = (picked[:, 0:queries] + shift_ref[...]) * log2e
     size[...] = size_ref[...] * log2e
     grads[:, queries:] = picked[:, queries:] * log2e
-    blocks = jnp.concatenate([p0[...], p1[...], p2[...], p3[...]], axis=0)
     eye = one_hot(iota((negatives, negatives), 0) == iota((negatives, negatives), 1))
-    columns = dot(blocks, eye, 0, 0) * log2e
+    columns = dot(block_ref[...], eye, 0, 0) * log2e
     high = columns.astype(bf16)
     entity[:, 0:negatives] = high
     entity[:, negatives:] = (columns - high.astype(f32)).astype(bf16)
@@ -365,8 +434,7 @@
 def gradients(slot, back, shift, size, blocks):
     width, queries = shift.shape
     rows = back.shape[0]
-    pool = blocks[0].shape[0]
-    negatives = 4 * pool
+    negatives = blocks.shape[0]
     padded = -(-width // lanes) * lanes
     work = negatives * queries * width
     return pl.pallas_call(
@@ -375,7 +443,7 @@
             jax.ShapeDtypeStruct((rows, padded), jnp.int16),
             jax.ShapeDtypeStruct((negatives, width), f32),
         ),
-        in_specs=[whole()] * 8,
+        in_specs=[whole()] * 5,
         out_specs=(whole(), whole()),
         scratch_shapes=[
             pltpu.VMEM((width, 2 * negatives), bf16),
@@ -395,7 +463,7 @@
             flops=16 * work, bytes_accessed=4 * rows * width, transcendentals=3 * work
         ),
         name="gradients",
-    )(slot, back, shift, size, *blocks)
+    )(slot, back, shift, size, blocks)
 
 
 def scatter_kernel(slot_count, asked_ref, neg_ref, back_ref, own_ref, q1, q2, q3, out_ref, column, rows_of, both):
@@ -407,10 +475,7 @@
     @pl.when(step == 0)
     def _():
         column[0:rows, :] = asked_column(asked_ref[...], slot_count)
-        here = iota((pool, pool), 0) == iota((pool, pool), 1)
-        column[rows : rows + pool, :] = jnp.sum(
-            jnp.where(here, neg_ref[...].astype(f32), 0.0), axis=1, keepdims=True
-        ).astype(i32)
+        column[rows : rows + pool, :] = column_of(neg_ref[...])
         column[rows + pool :, :] = jnp.full((lanes - pool, 1), -1, i32)
         level = back_ref[...].astype(i32).astype(f32)
         rows_of[0:rows, :] = level * jnp.exp2(-level[:, width : width + 1])
@@ -468,15 +533,14 @@
     )
     table = entity_table.T
     neg_row = neg_rows.reshape(1, pool)
-    wanted, slot = plan_slots(
-        entity_owner[:, :, 0].T, entity_row.T, slot_count, devices
-    )
-    asked = exchange(wanted.reshape(devices, 1, lanes)).reshape(devices, lanes)
-    served, block = serve(asked, neg_row, table, slot_count)
-    back = exchange(served.reshape(devices, slot_count, width)).reshape(-1, width)
-    shift, size = relations(rel_ids.T, query_type.reshape(1, queries), rel_center.T, rel_offset.T)
-    blocks = [block] + [shifted(block, "blk", step) for step in range(1, group_size)]
-    slot_grads, pool_grads = gradients(slot, back, shift, size, blocks)
+    slot, asked, back, blocks, shift, size = fetch(
+        entity_owner[:, :, 0].T, entity_row.T, neg_row, rel_ids.T, query_type.reshape(1, queries),
+        table, rel_center.T, rel_offset.T, slot_count, table_size, group_size,
+    )
+    asked = asked.reshape(devices, lanes)
+    slot_grads, pool_grads = gradients(
+        slot, back.reshape(-1, width), shift, size, blocks.reshape(-1, width)
+    )
     padded = slot_grads.shape[1]
     returned = exchange(slot_grads.reshape(devices, slot_count, padded)).reshape(-1, padded)
     others = [

time: 137 us -> 121 us (0.88)
  blocking collectives: 21 us -> 0 us
  Pallas kernels: 74.8 us -> 91.9 us
  starting transfers between devices: 21.4 us -> 10.1 us
  waiting for transfers between devices: 15.9 us -> 14.1 us
    all_to_all x1 -> x0, blocking collectives: 21 us -> none  [local(): asked = exchange(wanted.reshape(devices, 1, lanes)).reshape(devices, lanes)]
    pallas_call x3 -> x1, Pallas kernels: 21.7 us -> 38.7 us  [fetch(): pl.pallas_call(functools.partial(fetch_kernel, slot_count, table_size, gr...]
    ppermute x6 -> x3, starting transfers between devices: 9.81 us -> 5.42 us  [shifted(): return lax.ppermute(value, axis, pairs)]
    all_to_all x1 -> x0, starting transfers between devices: 4.25 us -> none  [local(): exchange(served.reshape(devices, slot_count, width)).reshape(-1, width)]
    all_to_all x1, starting transfers between devices: 7.28 us -> 4.64 us  [local(): exchange(slot_grads.reshape(devices, slot_count, padded))]
    all_to_all x1 -> x0, waiting for transfers between devices: 1.89 us -> none  [local(): exchange(served.reshape(devices, slot_count, width)).reshape(-1, width)]
    ppermute x6 -> x3, waiting for transfers between devices: 12.7 us -> 12.5 us  [shifted(): return lax.ppermute(value, axis, pairs)]
  transfers between devices with their start and end apart: 8 -> 4, of which waited for: 4 -> 3; matrix products, arithmetic and copies ran while one was open for 0% -> 0% of each run, Pallas kernels for 10% -> 0%
where the time goes in v2:
time: 121 us
  Pallas kernels  91.9 us (76%)
  waiting for transfers between devices  14.1 us (12%)
  starting transfers between devices  10.1 us (8%)
  local copies, waits for them, and re-layouts  4.62 us (4%)
    pallas_call x1, Pallas kernels, gradients(): pl.pallas_call(grads_kernel, out_shape=(jax.ShapeDtypeStruct((rows, padde...  40.8 us
    pallas_call x1, Pallas kernels, fetch(): pl.pallas_call(functools.partial(fetch_kernel, slot_count, table_size, gr...  38.7 us
    ppermute x3, waiting for transfers between devices, shifted(): return lax.ppermute(value, axis, pairs)  12.5 us
    pallas_call x1, Pallas kernels, scatter(): pl.pallas_call(functools.partial(scatter_kernel, slot_count), out_shape=j...  12.5 us
    ppermute x3, starting transfers between devices, shifted(): return lax.ppermute(value, axis, pairs)  5.42 us
    all_to_all x1, starting transfers between devices, local(): exchange(slot_grads.reshape(devices, slot_count, padded))  4.64 us
    unnamed x13, local copies, waits for them, and re-layouts  4.6 us
  transfers between devices with their start and end apart: 4, of which 3 were waited for; matrix products, arithmetic and copies ran while one was open for 0% of the time, Pallas kernels for 0%

profile of v2, /device:TPU:1, one launch (start us, length us, event | category | flops | bytes accessed | tf_op | source)
XLA Modules:
  0.0 120.8 jit_solution(996011546707445723)
XLA Ops:
  0.0 0.7 copy.11
  0.7 0.0 copy-start
  0.7 0.7 copy-done
  1.4 0.0 copy-start.1
  1.4 0.7 copy-done.1
  2.0 0.0 copy-start.3
  2.0 0.7 copy-done.3
  2.7 0.0 copy-start.4
  2.7 0.7 copy-done.4
  3.4 38.7 %fetch.1 = (s32[1,512]{1,0:T(1,128)S(1)}, f32[16,8,128]{2,1,0:T(8,128)S(1)}, bf16[128,8,400]{2,1,0:T(8,128)(2,1)}, bf16[4,32,400]{2,1,0:T(8,128)(2,1)S(1)}, f32[...) custom-call(s32[2,256]{1,0:T(2,128)S(1)} %bitcast.20, s32[2,256]{1,0:T(2,128)S(1)} %bitcast.24, s32[1,32]{1,0:T(1,128)S(1)} %bitcast.22, ...), custom_call_target="tpu_custom_call" | custom-call | tf_op jit(solution)/shard_map/fetch/pallas_call | solution.py:281
  42.1 0.0 copy-start.5
  42.1 1.2 %copy-done.5 = bf16[128,8,400]{2,1,0:T(8,128)(2,1)S(1)} copy-done((bf16[128,8,400]{2,1,0:T(8,128)(2,1)S(1)}, bf16[128,8,400]{2,1,0:T(8,128)(2,1)}, u32[]{:S(2)}) %copy-start.5) | copy-done | bytes 819224
  43.3 0.0 copy-start.2
  43.3 40.8 %gradients.1 = (s16[1024,512]{1,0:T(8,128)(2,1)}, f32[128,400]{1,0:T(8,128)S(1)}) custom-call(s32[1,512]{1,0:T(1,128)S(1)} %get-tuple-element.14.slot_ref, bf16[1024,400]{1,0:T(8,128)(2,1)S(1)} %bitcast.26, f32[400,256]{1,0:T(8,128)S(1)} %get-tuple-element.16.shift_ref, f32[400,256]{1,0:T(8,128)S(1)} %get-tuple-element.17.size_ref, bf16[128,400]{1,0:T(8,128)(2,1)S(1)} %bitcast.27), custom_call_target="tpu_custom_call" | custom-call | flops 209715200 | bytes 1638400 | tf_op jit(solution)/shard_map/gradients/pallas_call | solution.py:440
  84.1 4.6 %all-to-all-start = ((s16[128,8,512]{2,1,0:T(8,128)(2,1)}), s16[128,8,512]{2,1,0:T(8,128)(2,1)S(1)}, u32[]{:S(2)}, u32[]{:S(2)}) async-start(s16[128,8,512]{2,1,0:T(8,128)(2,1)} %bitcast.11), calls=%async_computation | async-start | bytes 2097152 | tf_op jit(solution)/shard_map/all_to_all | solution.py:545
  88.8 1.6 %collective-permute-start.2 = (f32[32,400]{1,0:T(8,128)S(1)}, f32[32,400]{1,0:T(8,128)S(1)}, u32[]{:S(2)}, u32[]{:S(2)}) collective-permute-start(f32[32,400]{1,0:T(8,128)S(1)} %get-tuple-element.21), channel_id=1, source_target_pairs={{0,1},{1,2},{2,3},{3,0},{4,5},{5,6},{6,7},{7,4},{8,9},{9,10},{10,1... | collective-permute-start | bytes 153608 | tf_op jit(solution)/shard_map/ppermute | solution.py:48
  90.3 2.9 %collective-permute-start.1 = (f32[32,400]{1,0:T(8,128)S(1)}, f32[32,400]{1,0:T(8,128)S(1)}, u32[]{:S(2)}, u32[]{:S(2)}) collective-permute-start(f32[32,400]{1,0:T(8,128)S(1)} %get-tuple-element.22), channel_id=1, source_target_pairs={{0,2},{1,3},{2,0},{3,1},{4,6},{5,7},{6,4},{7,5},{8,10},{9,11},{10,... | collective-permute-start | bytes 153608 | tf_op jit(solution)/shard_map/ppermute | solution.py:48
  93.3 0.9 collective-permute-start
  94.2 7.7 %collective-permute-done.2.q3 = f32[32,400]{1,0:T(8,128)S(1)} collective-permute-done((f32[32,400]{1,0:T(8,128)S(1)}, f32[32,400]{1,0:T(8,128)S(1)}, u32[]{:S(2)}, u32[]{:S(2)}) %collective-permute-start.2) | collective-permute-done | bytes 51232 | tf_op jit(solution)/shard_map/ppermute | solution.py:48
  101.9 4.8 %collective-permute-done.1.q2 = f32[32,400]{1,0:T(8,128)S(1)} collective-permute-done((f32[32,400]{1,0:T(8,128)S(1)}, f32[32,400]{1,0:T(8,128)S(1)}, u32[]{:S(2)}, u32[]{:S(2)}) %collective-permute-start.1) | collective-permute-done | bytes 51232 | tf_op jit(solution)/shard_map/ppermute | solution.py:48
  106.7 0.0 collective-permute-done.q1
  106.7 1.6 %all-to-all-done = s16[128,8,512]{2,1,0:T(8,128)(2,1)S(1)} async-done(((s16[128,8,512]{2,1,0:T(8,128)(2,1)}), s16[128,8,512]{2,1,0:T(8,128)(2,1)S(1)}, u32[]{:S(2)}, u32[]{:S(2)}) %all-to-all-start) | async-done | bytes 1048608 | tf_op jit(solution)/shard_map/all_to_all | solution.py:545
  108.3 0.0 copy-done.2
  108.3 12.5 %scatter.1 = f32[400,4096]{1,0:T(8,128)} custom-call(f32[128,128]{1,0:T(8,128)S(1)} %bitcast.19, s32[1,32]{1,0:T(1,128)S(1)} %bitcast.23, s16[1024,512]{1,0:T(8,128)(2,1)S(1)} %bitcast.18, f32[32,400]{1,0:T(8,128)S(1)} %get-tuple-element.24.own_ref, f32[32,400]{1,0:T(8,128)S(1)} %collective-permute-done.q1, f32[32,400]{1,0:T(8,128)S(1)} %collective-permute-done.1.q2, ...), custom_call_target="tpu_custom_call" | custom-call | tf_op jit(solution)/shard_map/scatter/pallas_call | solution.py:499
  (1 shorter events, 0.0 us)
Async XLA Ops:
  0.7 0.7 copy-start
  1.4 0.7 copy-start.1
  2.0 0.7 copy-start.3
  2.7 0.7 copy-start.4
  42.1 1.2 %copy-start.5 = (bf16[128,8,400]{2,1,0:T(8,128)(2,1)S(1)}, bf16[128,8,400]{2,1,0:T(8,128)(2,1)}, u32[]{:S(2)}) copy-start(bf16[128,8,400]{2,1,0:T(8,128)(2,1)} %get-tuple-element.15) | copy-start | bytes 2457604
  43.3 65.0 %copy-start.2 = (s32[32]{0:T(128)S(1)}, s32[32]{0:T(128)}, u32[]{:S(2)}) copy-start(s32[32]{0:T(128)} %param.15) | copy-start | bytes 388
  84.1 24.2 %all-to-all-start = ((s16[128,8,512]{2,1,0:T(8,128)(2,1)}), s16[128,8,512]{2,1,0:T(8,128)(2,1)S(1)}, u32[]{:S(2)}, u32[]{:S(2)}) async-start(s16[128,8,512]{2,1,0:T(8,128)(2,1)} %bitcast.11), calls=%async_computation | async-start | bytes 2097152 | tf_op jit(solution)/shard_map/all_to_all | solution.py:545
  88.8 13.1 %collective-permute-start.2 = (f32[32,400]{1,0:T(8,128)S(1)}, f32[32,400]{1,0:T(8,128)S(1)}, u32[]{:S(2)}, u32[]{:S(2)}) collective-permute-start(f32[32,400]{1,0:T(8,128)S(1)} %get-tuple-element.21), channel_id=1, source_target_pairs={{0,1},{1,2},{2,3},{3,0},{4,5},{5,6},{6,7},{7,4},{8,9},{9,10},{10,1... | collective-permute-start | bytes 153608 | tf_op jit(solution)/shard_map/ppermute | solution.py:48
  90.3 16.3 %collective-permute-start.1 = (f32[32,400]{1,0:T(8,128)S(1)}, f32[32,400]{1,0:T(8,128)S(1)}, u32[]{:S(2)}, u32[]{:S(2)}) collective-permute-start(f32[32,400]{1,0:T(8,128)S(1)} %get-tuple-element.22), channel_id=1, source_target_pairs={{0,2},{1,3},{2,0},{3,1},{4,6},{5,7},{6,4},{7,5},{8,10},{9,11},{10,... | collective-permute-start | bytes 153608 | tf_op jit(solution)/shard_map/ppermute | solution.py:48
  93.3 13.4 %collective-permute-start = (f32[32,400]{1,0:T(8,128)S(1)}, f32[32,400]{1,0:T(8,128)S(1)}, u32[]{:S(2)}, u32[]{:S(2)}) collective-permute-start(f32[32,400]{1,0:T(8,128)S(1)} %get-tuple-element.23), channel_id=1, source_target_pairs={{0,3},{1,0},{2,1},{3,2},{4,7},{5,4},{6,5},{7,6},{8,11},{9,8},{10,9... | collective-permute-start | bytes 153608 | tf_op jit(solution)/shard_map/ppermute | solution.py:48

commit v3 on v2

--- a/solution.py
+++ b/solution.py
@@ -42,18 +42,12 @@
     return pltpu.CompilerParams(vmem_limit_bytes=mib * 2**20, **more)
 
 
-def shifted(value, axis, steps):
-    count = lax.axis_size(axis)
-    pairs = [(source, (source + steps) % count) for source in range(count)]
-    return lax.ppermute(value, axis, pairs)
-
-
 def one_hot(mask):
     return jnp.where(mask, 1.0, 0.0).astype(bf16)
 
 
 def plan_slots(owner_ref, row_ref, slot_count, devices, mates):
-    owner = jnp.concatenate([owner_ref[0:1, :], owner_ref[1:2, :]], axis=1)
+    owner = jnp.concatenate([owner_ref[0], owner_ref[1]], axis=1)
     row = jnp.concatenate([row_ref[0:1, :], row_ref[1:2, :]], axis=1)
     requests = owner.shape[1]
     bits = int(math.log2(mates))
@@ -95,9 +89,9 @@
 
 def fetch_kernel(
     slot_count, table_size, group_size,
-    owner_ref, row_ref, neg_ref, ids_ref, type_ref, table_hbm, center_hbm, offset_hbm,
-    slot_ref, asked_ref, back_ref, block_ref, shift_ref, size_ref,
-    table, center_tab, offset_tab, center_sum, offset_rows, wanted, passed, ordered, served, column,
+    owner_hbm, row_hbm, neg_hbm, ids_hbm, type_hbm, table_hbm, center_hbm, offset_hbm,
+    asked_ref, slot_ref, back_ref, block_ref, shift_ref, size_ref,
+    owner_ref, row_ref, neg_ref, ids_ref, type_ref, table, center_tab, offset_tab, center_sum, offset_rows, wanted, passed, ordered, served, column,
     load_sems, first_send, first_recv, second_send, second_recv, row_send, row_recv,
     pool_send, pool_recv,
 ):
@@ -117,10 +111,14 @@
     loads = [
         pltpu.make_async_copy(source, place, load_sems.at[i])
         for i, (source, place) in enumerate(
-            [(table_hbm, table), (center_hbm, center_tab), (offset_hbm, offset_tab)]
+            [
+                (table_hbm, table), (center_hbm, center_tab), (offset_hbm, offset_tab),
+                (owner_hbm, owner_ref), (row_hbm, row_ref), (neg_hbm, neg_ref),
+                (ids_hbm, ids_ref), (type_hbm, type_ref),
+            ]
         )
     ]
-    for load in loads:
+    for load in loads[3:] + loads[:3]:
         load.start()
 
     barrier = pltpu.get_barrier_semaphore()
@@ -133,6 +131,8 @@
 
     lax.fori_loop(1, devices, greet, 0)
 
+    for load in loads[3:]:
+        load.wait()
     slot, asked = plan_slots(owner_ref, row_ref, slot_count, devices, mates)
     slot_ref[...] = slot
     wanted[...] = asked.reshape(mates, teams, lanes)
@@ -267,47 +267,6 @@
     await_all(back_ref, devices - 1, row_recv)
 
 
-def fetch(owner, row, neg_row, rel_ids, query_type, table, rel_center, rel_offset, slot_count,
-          table_size, group_size):
-    hops, queries = rel_ids.shape
-    width, rels = rel_center.shape
-    entities = table.shape[1]
-    devices = table_size * group_size
-    mates = 2 * group_size
-    teams = devices // mates
-    pool = neg_row.shape[1]
-    anywhere = pl.BlockSpec(memory_space=pl.ANY)
-    dma = pltpu.SemaphoreType.DMA
-    return pl.pallas_call(
-        functools.partial(fetch_kernel, slot_count, table_size, group_size),
-        out_shape=(
-            jax.ShapeDtypeStruct((1, 2 * queries), i32),
-            jax.ShapeDtypeStruct((teams, mates, lanes), f32),
-            jax.ShapeDtypeStruct((devices, slot_count, width), bf16),
-            jax.ShapeDtypeStruct((group_size, pool, width), bf16),
-            jax.ShapeDtypeStruct((width, queries), f32),
-            jax.ShapeDtypeStruct((width, queries), f32),
-        ),
-        in_specs=[whole()] * 5 + [anywhere] * 3,
-        out_specs=(whole(),) * 6,
-        scratch_shapes=[
-            pltpu.VMEM((width, entities), bf16),
-            pltpu.VMEM((width, rels), bf16),
-            pltpu.VMEM((width, rels), bf16),
-            pltpu.VMEM((width, queries), f32),
-            pltpu.VMEM((width, hops * queries), f32),
-            pltpu.VMEM((mates, teams, lanes), f32),
-            pltpu.VMEM((mates, teams, lanes), f32),
-            pltpu.VMEM((teams, mates, lanes), f32),
-            pltpu.VMEM((devices, slot_count, width), bf16),
-            pltpu.VMEM((devices * slot_count, 1), i32),
-            dma((3,)), dma, dma, dma, dma, dma, dma, dma((group_size,)), dma((group_size,)),
-        ],
-        compiler_params=params(52, collective_id=0, has_side_effects=True),
-        name="fetch",
-    )(owner, row, neg_row, rel_ids, query_type, table, rel_center, rel_offset)
-
-
 def slope_terms(gap, size):
     square = gap * gap + scaled_eps
     inverse = lax.rsqrt(square)
@@ -317,20 +276,27 @@
     return spread, above, slope
 
 
-def grads_kernel(slot_ref, back_ref, shift_ref, size_ref, block_ref, slots_ref, pool_ref,
-                 entity, picks, spread_out, center, size, grads, slopes, dists, weights, pool_grad, codes):
+def grads_kernel(table_size, group_size, slot_ref, back_ref, block_ref, shift_ref, size_ref,
+                 returned_ref, pool_ref, entity, picks, spread_out, center, size, grads, slopes, dists, weights, pool_grad, codes,
+                 coded, pool_rows, row_send, row_recv, pool_send, pool_recv):
     width, queries = shift_ref.shape
-    rows = back_ref.shape[0]
-    negatives = block_ref.shape[0]
+    rows = back_ref.shape[0] * back_ref.shape[1]
+    negatives = block_ref.shape[0] * block_ref.shape[1]
     tiles = width // 8
+    devices = table_size * group_size
+    row_me, col_me = lax.axis_index("table"), lax.axis_index("blk")
+    me = row_me * group_size + col_me
+
+    def target(index):
+        return (lax.div(index, group_size), lax.rem(index, group_size))
 
     hot = one_hot(iota((rows, 2 * queries), 0) == slot_ref[...])
-    picked = dot(back_ref[...], hot, 0, 0)
+    picked = dot(back_ref[...].reshape(rows, width), hot, 0, 0)
     center[...] = (picked[:, 0:queries] + shift_ref[...]) * log2e
     size[...] = size_ref[...] * log2e
     grads[:, queries:] = picked[:, queries:] * log2e
     eye = one_hot(iota((negatives, negatives), 0) == iota((negatives, negatives), 1))
-    columns = dot(block_ref[...], eye, 0, 0) * log2e
+    columns = dot(block_ref[...].reshape(negatives, width), eye, 0, 0) * log2e
     high = columns.astype(bf16)
     entity[:, 0:negatives] = high
     entity[:, negatives:] = (columns - high.astype(f32)).astype(bf16)
@@ -426,51 +392,134 @@
     codes[0:width, 0 : 2 * queries] = high.astype(bf16)
     codes[0:width, 2 * queries :] = low.astype(bf16)
     codes[width : width + 16, 2 * queries :] = jnp.broadcast_to(power, (16, 2 * queries)).astype(bf16)
-    level = dot(hot, codes[:, 0 : 2 * queries], 1, 1) * 256.0 + dot(hot, codes[:, 2 * queries :], 1, 1)
-    slots_ref[...] = level.astype(i32).astype(jnp.int16)
-    pool_ref[...] = jnp.transpose(pool_grad[...])[:, 0:width]
-
-
-def gradients(slot, back, shift, size, blocks):
-    width, queries = shift.shape
-    rows = back.shape[0]
-    negatives = blocks.shape[0]
+    for step in range(group_size):
+        pool_rows[step] = jnp.transpose(
+            pool_grad[...]
+        )[step * negatives // group_size : (step + 1) * negatives // group_size, 0:width]
+    copies = []
+    for step in range(1, group_size):
+        copy = pltpu.make_async_remote_copy(
+            src_ref=pool_rows.at[step], dst_ref=pool_ref.at[step],
+            send_sem=pool_send.at[step], recv_sem=pool_recv.at[step],
+            device_id=(row_me, lax.rem(col_me + group_size - step, group_size)),
+            device_id_type=MESH,
+        )
+        copy.start()
+        copies.append(copy)
+
+    slot_count = rows // devices
+    quarter = devices // 4
+    mine, inside = lax.div(me, quarter), lax.rem(me, quarter)
+    for turn in (1, 2, 3, 0):
+        part = lax.rem(mine + turn, 4)
+        size = quarter * slot_count
+        chosen = one_hot(iota((size, 2 * queries), 0) + part * size == slot_ref[...])
+        level = dot(chosen, codes[:, 0 : 2 * queries], 1, 1) * 256.0
+        level = level + dot(chosen, codes[:, 2 * queries :], 1, 1)
+        level = level.astype(i32).astype(jnp.int16)
+        coded[pl.ds(part * quarter, quarter)] = level.reshape(quarter, slot_count, codes.shape[0])
+
+        def send_rows(i, _):
+            other = part * quarter + lax.rem(inside + i, quarter)
+            pltpu.make_async_remote_copy(
+                src_ref=coded.at[other], dst_ref=returned_ref.at[me],
+                send_sem=row_send, recv_sem=row_recv,
+                device_id=target(other), device_id_type=MESH,
+            ).start()
+            return 0
+
+        lax.fori_loop(1 if turn == 0 else 0, quarter, send_rows, 0)
+
+    returned_ref[me] = coded[me]
+    pool_ref[0] = pool_rows[0]
+    for copy in copies:
+        copy.wait()
+    sent, got = coded.at[pl.ds(0, devices - 1)], returned_ref.at[pl.ds(0, devices - 1)]
+    pltpu.make_async_copy(sent, sent, row_send).wait()
+    pltpu.make_async_copy(got, got, row_recv).wait()
+
+
+def step_kernel(slot_count, table_size, group_size, *refs):
+    sources, (asked_ref, returned_ref, pool_ref), scratch = refs[0:8], refs[8:11], refs[11:]
+    boxes, fetching, grading = scratch[0:5], scratch[5:29], scratch[29:]
+    fetch_kernel(slot_count, table_size, group_size, *sources, asked_ref, *boxes, *fetching)
+    grads_kernel(table_size, group_size, *boxes, returned_ref, pool_ref, *grading)
+
+
+def step(owner, row, neg_row, rel_ids, query_type, table, rel_center, rel_offset, slot_count,
+         table_size, group_size):
+    hops, queries = rel_ids.shape
+    width, rels = rel_center.shape
+    entities = table.shape[1]
+    devices = table_size * group_size
+    mates = 2 * group_size
+    teams = devices // mates
+    pool = neg_row.shape[1]
+    negatives = group_size * pool
     padded = -(-width // lanes) * lanes
-    work = negatives * queries * width
+    dma = pltpu.SemaphoreType.DMA
+    boxes = [
+        pltpu.VMEM((1, 2 * queries), i32),
+        pltpu.VMEM((devices, slot_count, width), bf16),
+        pltpu.VMEM((group_size, pool, width), bf16),
+        pltpu.VMEM((width, queries), f32),
+        pltpu.VMEM((width, queries), f32),
+    ]
+    fetching = [
+        pltpu.VMEM(owner.shape, i32),
+        pltpu.VMEM(row.shape, i32),
+        pltpu.VMEM(neg_row.shape, i32),
+        pltpu.VMEM(rel_ids.shape, i32),
+        pltpu.VMEM(query_type.shape, i32),
+        pltpu.VMEM((width, entities), bf16),
+        pltpu.VMEM((width, rels), bf16),
+        pltpu.VMEM((width, rels), bf16),
+        pltpu.VMEM((width, queries), f32),
+        pltpu.VMEM((width, hops * queries), f32),
+        pltpu.VMEM((mates, teams, lanes), f32),
+        pltpu.VMEM((mates, teams, lanes), f32),
+        pltpu.VMEM((teams, mates, lanes), f32),
+        pltpu.VMEM((devices, slot_count, width), bf16),
+        pltpu.VMEM((devices * slot_count, 1), i32),
+        dma((8,)), dma, dma, dma, dma, dma, dma, dma((group_size,)), dma((group_size,)),
+    ]
+    grading = [
+        pltpu.VMEM((width, 2 * negatives), bf16),
+        pltpu.VMEM((2 * negatives, near * lanes), bf16),
+        pltpu.VMEM((2, width, near * lanes), f32),
+        pltpu.VMEM((width, queries), f32),
+        pltpu.VMEM((width, queries), f32),
+        pltpu.VMEM((width, 2 * queries), f32),
+        pltpu.VMEM((near, width, queries), f32),
+        pltpu.VMEM((near, queries), f32),
+        pltpu.VMEM((near, queries), f32),
+        pltpu.VMEM((padded, negatives), f32),
+        pltpu.VMEM((padded, 4 * queries), bf16),
+        pltpu.VMEM((devices, slot_count, padded), jnp.int16),
+        pltpu.VMEM((group_size, pool, width), f32),
+        dma, dma, dma((group_size,)), dma((group_size,)),
+    ]
+    scratch = boxes + fetching + grading
     return pl.pallas_call(
-        grads_kernel,
+        functools.partial(step_kernel, slot_count, table_size, group_size),
         out_shape=(
-            jax.ShapeDtypeStruct((rows, padded), jnp.int16),
-            jax.ShapeDtypeStruct((negatives, width), f32),
+            jax.ShapeDtypeStruct((teams, mates, lanes), f32),
+            jax.ShapeDtypeStruct((devices, slot_count, padded), jnp.int16),
+            jax.ShapeDtypeStruct((group_size, pool, width), f32),
         ),
-        in_specs=[whole()] * 5,
-        out_specs=(whole(), whole()),
-        scratch_shapes=[
-            pltpu.VMEM((width, 2 * negatives), bf16),
-            pltpu.VMEM((2 * negatives, near * lanes), bf16),
-            pltpu.VMEM((2, width, near * lanes), f32),
-            pltpu.VMEM((width, queries), f32),
-            pltpu.VMEM((width, queries), f32),
-            pltpu.VMEM((width, 2 * queries), f32),
-            pltpu.VMEM((near, width, queries), f32),
-            pltpu.VMEM((near, queries), f32),
-            pltpu.VMEM((near, queries), f32),
-            pltpu.VMEM((padded, negatives), f32),
-            pltpu.VMEM((padded, 4 * queries), bf16),
-        ],
-        compiler_params=params(48),
-        cost_estimate=pl.CostEstimate(
-            flops=16 * work, bytes_accessed=4 * rows * width, transcendentals=3 * work
-        ),
-        name="gradients",
-    )(slot, back, shift, size, blocks)
-
-
-def scatter_kernel(slot_count, asked_ref, neg_ref, back_ref, own_ref, q1, q2, q3, out_ref, column, rows_of, both):
+        in_specs=[pl.BlockSpec(memory_space=pltpu.HBM)] * 8,
+        out_specs=(whole(),) * 3,
+        scratch_shapes=scratch,
+        compiler_params=params(56, collective_id=0, has_side_effects=True),
+        name="step",
+    )(owner, row, neg_row, rel_ids, query_type, table, rel_center, rel_offset)
+
+
+def scatter_kernel(slot_count, asked_ref, neg_ref, back_ref, pool_ref, out_ref, column, rows_of, both):
     step = pl.program_id(0)
     width, part = out_ref.shape
     rows, padded = back_ref.shape
-    pool = q1.shape[0]
+    group_size, pool = pool_ref.shape[0:2]
 
     @pl.when(step == 0)
     def _():
@@ -480,21 +529,21 @@
         level = back_ref[...].astype(i32).astype(f32)
         rows_of[0:rows, :] = level * jnp.exp2(-level[:, width : width + 1])
         rows_of[rows:, :] = jnp.zeros((lanes, padded), f32)
-        rows_of[rows : rows + pool, 0:width] = own_ref[...] + q1[...] + q2[...] + q3[...]
+        rows_of[rows : rows + pool, 0:width] = sum(pool_ref[i] for i in range(group_size))
         value = jnp.transpose(rows_of[...])[0:width, :]
         high = value.astype(bf16)
         both[0:width, :] = high
         both[width:, :] = (value - high.astype(f32)).astype(bf16)
 
-    hot = one_hot(iota((rows + lanes, part), 1) + step * part == column[...])
+    hot = one_hot(iota((rows + lanes, part), 1) == column[...] - step * part)
     result = dot(both[...], hot, 1, 0)
     out_ref[...] = result[0:width, :] + result[width:, :]
 
 
-def scatter(asked, neg_rows, back, own, others, slot_count, entities):
+def scatter(asked, neg_rows, back, pools, slot_count, entities):
     rows, padded = back.shape
-    pool, width = own.shape
-    part = 512
+    width = pools.shape[2]
+    part = 1024
     fixed = lambda i: (0, 0)
     return pl.pallas_call(
         functools.partial(scatter_kernel, slot_count),
@@ -504,8 +553,8 @@
             pl.BlockSpec(asked.shape, fixed),
             pl.BlockSpec(neg_rows.shape, fixed),
             pl.BlockSpec((rows, padded), fixed),
-        ]
-        + [pl.BlockSpec((pool, width), fixed)] * 4,
+            pl.BlockSpec(pools.shape, lambda i: (0, 0, 0)),
+        ],
         out_specs=pl.BlockSpec((width, part), lambda i: (0, i)),
         scratch_shapes=[
             pltpu.VMEM((rows + lanes, 1), i32),
@@ -514,7 +563,7 @@
         ],
         compiler_params=params(48),
         name="scatter",
-    )(asked, neg_rows, back, own, *others)
+    )(asked, neg_rows, back, pools)
 
 
 def local(
@@ -527,29 +576,16 @@
     queries = rel_ids.shape[0]
     slot_count = 4 * queries // devices
     pool = neg_rows.shape[0]
-    axes = ("table", "blk")
-    exchange = functools.partial(
-        lax.all_to_all, axis_name=axes, split_axis=0, concat_axis=0, tiled=True
-    )
     table = entity_table.T
     neg_row = neg_rows.reshape(1, pool)
-    slot, asked, back, blocks, shift, size = fetch(
-        entity_owner[:, :, 0].T, entity_row.T, neg_row, rel_ids.T, query_type.reshape(1, queries),
-        table, rel_center.T, rel_offset.T, slot_count, table_size, group_size,
+    asked, returned, pool_grads = step(
+        entity_owner.transpose(1, 2, 0), entity_row.T, neg_row, rel_ids.T,
+        query_type.reshape(1, queries), table, rel_center.T, rel_offset.T, slot_count,
+        table_size, group_size,
     )
     asked = asked.reshape(devices, lanes)
-    slot_grads, pool_grads = gradients(
-        slot, back.reshape(-1, width), shift, size, blocks.reshape(-1, width)
-    )
-    padded = slot_grads.shape[1]
-    returned = exchange(slot_grads.reshape(devices, slot_count, padded)).reshape(-1, padded)
-    others = [
-        shifted(pool_grads[step * pool : (step + 1) * pool], "blk", -step)
-        for step in range(1, group_size)
-    ]
-    return scatter(
-        asked, neg_row, returned, pool_grads[0:pool], others, slot_count, entities
-    ).T
+    returned = returned.reshape(devices * slot_count, -1)
+    return scatter(asked, neg_row, returned, pool_grads, slot_count, entities).T
 
 
 def solution(mesh):

time: 121 us -> 110 us (0.909)
  Pallas kernels: 91.9 us -> 107 us
  waiting for transfers between devices: 14.1 us -> 0 us
  starting transfers between devices: 10.1 us -> 0 us
  local copies, waits for them, and re-layouts: 4.62 us -> 3.01 us
    pallas_call x2 -> x1, Pallas kernels: 79.5 us -> 95 us  [step(): pl.pallas_call(functools.partial(step_kernel, slot_count, table_size, gro...]
    ppermute x3 -> x0, waiting for transfers between devices: 12.5 us -> none  [shifted(): return lax.ppermute(value, axis, pairs)]
    ppermute x3 -> x0, starting transfers between devices: 5.42 us -> none  [shifted(): return lax.ppermute(value, axis, pairs)]
    all_to_all x1 -> x0, starting transfers between devices: 4.64 us -> none  [local(): exchange(slot_grads.reshape(devices, slot_count, padded))]
    all_to_all x1 -> x0, waiting for transfers between devices: 1.64 us -> none  [local(): exchange(slot_grads.reshape(devices, slot_count, padded))]
    unnamed x13 -> x8, local copies, waits for them, and re-layouts: 4.6 us -> 3.01 us
  transfers between devices with their start and end apart: 4 -> 0, of which waited for: 3 -> 0; matrix products, arithmetic and copies ran while one was open for 0% -> 0% of each run, Pallas kernels for 0% -> 0%
where the time goes in v3:
time: 110 us
  Pallas kernels  107 us (97%)
  local copies, waits for them, and re-layouts  3.01 us (3%)
    pallas_call x1, Pallas kernels, step(): pl.pallas_call(functools.partial(step_kernel, slot_count, table_size, gro...  95 us
    pallas_call x1, Pallas kernels, scatter(): pl.pallas_call(functools.partial(scatter_kernel, slot_count), out_shape=j...  11.8 us
    unnamed x8, local copies, waits for them, and re-layouts  3.01 us

profile of v3, /device:TPU:1, one launch (start us, length us, event | category | flops | bytes accessed | tf_op | source)
XLA Modules:
  0.0 109.8 jit_solution(12884223769929351918)
XLA Ops:
  0.0 0.0 copy-start.3
  0.0 95.0 %step.1 = (f32[16,8,128]{2,1,0:T(8,128)}, s16[128,8,512]{2,1,0:T(8,128)(2,1)}, f32[4,32,400]{2,1,0:T(8,128)}) custom-call(s32[2,1,256]{2,1,0:T(1,128)} %bitcast.19, s32[2,256]{1,0:T(2,128)} %bitcast.20, s32[1,32]{1,0:T(1,128)} %bitcast.13, s32[3,256]{1,0:T(4,128)} %bitcast.18, s32[1,256]{1,0:T(1,128)} %bitcast.21, bf16[400,4096]{1,0:T(8,128)(2,1)} %bitcast.17, ...), custom_call_target="tpu_custom_call" | custom-call | tf_op jit(solution)/shard_map/step/pallas_call | solution.py:503
  95.0 0.0 copy-done.3
  95.0 0.0 copy-start
  95.0 1.2 %copy-done = s16[128,8,512]{2,1,0:T(8,128)(2,1)S(1)} copy-done((s16[128,8,512]{2,1,0:T(8,128)(2,1)S(1)}, s16[128,8,512]{2,1,0:T(8,128)(2,1)}, u32[]{:S(2)}) %copy-start) | copy-done | bytes 1048600
  96.2 0.0 copy-start.1
  96.3 0.9 copy-done.1
  97.2 0.0 copy-start.2
  97.2 0.8 copy-done.2
  98.0 11.8 %scatter.1 = f32[400,4096]{1,0:T(8,128)} custom-call(f32[128,128]{1,0:T(8,128)S(1)} %bitcast.12, s32[1,32]{1,0:T(1,128)S(1)} %bitcast.14, s16[1024,512]{1,0:T(8,128)(2,1)S(1)} %bitcast.11, f32[4,32,400]{2,1,0:T(8,128)S(1)} %copy-done.1), custom_call_target="tpu_custom_call" | custom-call | tf_op jit(solution)/shard_map/scatter/pallas_call | solution.py:548
Async XLA Ops:
  0.0 95.0 %copy-start.3 = (s32[32]{0:T(128)S(1)}, s32[32]{0:T(128)}, u32[]{:S(2)}) copy-start(s32[32]{0:T(128)} %param.15) | copy-start | bytes 388
  95.0 1.2 %copy-start = (s16[128,8,512]{2,1,0:T(8,128)(2,1)S(1)}, s16[128,8,512]{2,1,0:T(8,128)(2,1)}, u32[]{:S(2)}) copy-start(s16[128,8,512]{2,1,0:T(8,128)(2,1)} %get-tuple-element.9) | copy-start | bytes 3145732
  96.2 0.9 copy-start.1
  97.2 0.8 copy-start.2

commit v4 on v3

--- a/solution.py
+++ b/solution.py
@@ -65,10 +65,32 @@
     return owner * slot_count + rank, dot(named_hot, parts.astype(bf16), 1, 1)
 
 
-def asked_column(asked, slot_count):
+def partner(position, row_me, col_me):
+    def part(value, size):
+        return value - lax.div(value, jnp.full_like(value, size)) * size
+
+    def over(value, size):
+        return lax.div(value, jnp.full_like(value, size))
+
+    core, depth, rest = part(position, 2), part(over(position, 2), 4), over(position, 8)
+    line, plane = part(rest, 4), over(rest, 4)
+    y = part(over(row_me, 2) + line + depth, 4)
+    x = part(over(row_me, 8) + plane + depth + 2 * line, 4)
+    core = part(row_me + core, 2)
+    return (x * 4 + y) * 2 + core, part(col_me + depth, 4)
+
+
+def partner_index(position, row_me, col_me, group_size):
+    row, col = partner(position, row_me, col_me)
+    return row * group_size + col
+
+
+def asked_column(asked, slot_count, order=None):
     devices = asked.shape[0]
     rows = devices * slot_count
-    group = lax.shift_right_logical(iota((rows, devices), 0), int(math.log2(slot_count)))
+    group = lax.shift_right_logical(iota((rows, 1), 0), int(math.log2(slot_count)))
+    if order is not None:
+        group = order(group)
     pick = one_hot(group == iota((rows, devices), 1))
     spread = dot(pick, asked.astype(bf16), 1, 0)
     slot = iota((rows, lanes), 0) & (slot_count - 1)
@@ -230,27 +252,27 @@
     await_all(ordered, teams - 1, second_send)
     await_all(asked_ref, teams - 1, second_recv)
 
-    column[...] = asked_column(asked_ref[...].reshape(devices, lanes), slot_count)
+    column[...] = asked_column(
+        asked_ref[...].reshape(devices, lanes), slot_count,
+        lambda group: partner_index(group, row_me, col_me, group_size),
+    )
     quarter = devices // 4
-    mine, inside = lax.div(me, quarter), lax.rem(me, quarter)
-    for turn in (1, 2, 3, 0):
-        part = lax.rem(mine + turn, 4)
+
+    def send_rows(i, _):
+        pltpu.make_async_remote_copy(
+            src_ref=served.at[i], dst_ref=back_ref.at[me],
+            send_sem=row_send, recv_sem=row_recv,
+            device_id=partner(i, row_me, col_me), device_id_type=MESH,
+        ).start()
+        return 0
+
+    for part in (1, 2, 3, 0):
         size = quarter * slot_count
-        rows = rows_at(column[pl.ds(pl.multiple_of(part * size, size), size), :])
-        served[pl.ds(part * quarter, quarter)] = rows.reshape(quarter, slot_count, width)
-
-        def send_rows(i, _):
-            other = part * quarter + lax.rem(inside + i, quarter)
-            pltpu.make_async_remote_copy(
-                src_ref=served.at[other], dst_ref=back_ref.at[me],
-                send_sem=row_send, recv_sem=row_recv,
-                device_id=target(other), device_id_type=MESH,
-            ).start()
-            return 0
-
-        lax.fori_loop(1 if turn == 0 else 0, quarter, send_rows, 0)
-
-    back_ref[me] = served[me]
+        rows = rows_at(column[part * size : (part + 1) * size, :])
+        served[part * quarter : (part + 1) * quarter] = rows.reshape(quarter, slot_count, width)
+        lax.fori_loop(max(1, part * quarter), (part + 1) * quarter, send_rows, 0)
+
+    back_ref[me] = served[0]
     relations_part(1)
     relations_part(2)
     if rels % step:
@@ -409,28 +431,32 @@
 
     slot_count = rows // devices
     quarter = devices // 4
-    mine, inside = lax.div(me, quarter), lax.rem(me, quarter)
-    for turn in (1, 2, 3, 0):
-        part = lax.rem(mine + turn, 4)
+
+    def send_rows(i, _):
+        pltpu.make_async_remote_copy(
+            src_ref=coded.at[i], dst_ref=returned_ref.at[me],
+            send_sem=row_send, recv_sem=row_recv,
+            device_id=partner(i, row_me, col_me), device_id_type=MESH,
+        ).start()
+        return 0
+
+    for part in range(4):
         size = quarter * slot_count
-        chosen = one_hot(iota((size, 2 * queries), 0) + part * size == slot_ref[...])
+        place = iota((size, 1), 0) + part * size
+        group = lax.shift_right_logical(place, int(math.log2(slot_count)))
+        place = (place & (slot_count - 1)) + slot_count * partner_index(
+            group, row_me, col_me, group_size
+        )
+        chosen = one_hot(place == slot_ref[...])
         level = dot(chosen, codes[:, 0 : 2 * queries], 1, 1) * 256.0
         level = level + dot(chosen, codes[:, 2 * queries :], 1, 1)
         level = level.astype(i32).astype(jnp.int16)
-        coded[pl.ds(part * quarter, quarter)] = level.reshape(quarter, slot_count, codes.shape[0])
-
-        def send_rows(i, _):
-            other = part * quarter + lax.rem(inside + i, quarter)
-            pltpu.make_async_remote_copy(
-                src_ref=coded.at[other], dst_ref=returned_ref.at[me],
-                send_sem=row_send, recv_sem=row_recv,
-                device_id=target(other), device_id_type=MESH,
-            ).start()
-            return 0
-
-        lax.fori_loop(1 if turn == 0 else 0, quarter, send_rows, 0)
-
-    returned_ref[me] = coded[me]
+        coded[part * quarter : (part + 1) * quarter] = level.reshape(
+            quarter, slot_count, codes.shape[0]
+        )
+        lax.fori_loop(max(1, part * quarter), (part + 1) * quarter, send_rows, 0)
+
+    returned_ref[me] = coded[0]
     pool_ref[0] = pool_rows[0]
     for copy in copies:
         copy.wait()
@@ -515,7 +541,8 @@
     )(owner, row, neg_row, rel_ids, query_type, table, rel_center, rel_offset)
 
 
-def scatter_kernel(slot_count, asked_ref, neg_ref, back_ref, pool_ref, out_ref, column, rows_of, both):
+def scatter_kernel(slot_count, asked_hbm, neg_hbm, back_hbm, pool_hbm, out_ref,
+                   asked_ref, neg_ref, back_ref, pool_ref, column, rows_of, both, sems):
     step = pl.program_id(0)
     width, part = out_ref.shape
     rows, padded = back_ref.shape
@@ -523,12 +550,27 @@
 
     @pl.when(step == 0)
     def _():
+        loads = [
+            pltpu.make_async_copy(source, place, sems.at[i])
+            for i, (source, place) in enumerate(
+                [
+                    (asked_hbm, asked_ref), (neg_hbm, neg_ref), (back_hbm, back_ref),
+                    (pool_hbm, pool_ref),
+                ]
+            )
+        ]
+        for load in loads:
+            load.start()
+        loads[0].wait()
         column[0:rows, :] = asked_column(asked_ref[...], slot_count)
+        loads[1].wait()
         column[rows : rows + pool, :] = column_of(neg_ref[...])
         column[rows + pool :, :] = jnp.full((lanes - pool, 1), -1, i32)
+        loads[2].wait()
         level = back_ref[...].astype(i32).astype(f32)
         rows_of[0:rows, :] = level * jnp.exp2(-level[:, width : width + 1])
         rows_of[rows:, :] = jnp.zeros((lanes, padded), f32)
+        loads[3].wait()
         rows_of[rows : rows + pool, 0:width] = sum(pool_ref[i] for i in range(group_size))
         value = jnp.transpose(rows_of[...])[0:width, :]
         high = value.astype(bf16)
@@ -542,26 +584,26 @@
 
 def scatter(asked, neg_rows, back, pools, slot_count, entities):
     rows, padded = back.shape
+    pool = neg_rows.shape[1]
     width = pools.shape[2]
     part = 1024
-    fixed = lambda i: (0, 0)
     return pl.pallas_call(
         functools.partial(scatter_kernel, slot_count),
         out_shape=jax.ShapeDtypeStruct((width, entities), f32),
         grid=(entities // part,),
-        in_specs=[
-            pl.BlockSpec(asked.shape, fixed),
-            pl.BlockSpec(neg_rows.shape, fixed),
-            pl.BlockSpec((rows, padded), fixed),
-            pl.BlockSpec(pools.shape, lambda i: (0, 0, 0)),
-        ],
+        in_specs=[pl.BlockSpec(memory_space=pltpu.HBM)] * 4,
         out_specs=pl.BlockSpec((width, part), lambda i: (0, i)),
         scratch_shapes=[
+            pltpu.VMEM(asked.shape, f32),
+            pltpu.VMEM(neg_rows.shape, i32),
+            pltpu.VMEM(back.shape, jnp.int16),
+            pltpu.VMEM(pools.shape, f32),
             pltpu.VMEM((rows + lanes, 1), i32),
             pltpu.VMEM((rows + lanes, padded), f32),
             pltpu.VMEM((2 * width, rows + lanes), bf16),
+            pltpu.SemaphoreType.DMA((4,)),
         ],
-        compiler_params=params(48),
+        compiler_params=params(56),
         name="scatter",
     )(asked, neg_rows, back, pools)
 

time: 110 us -> 107 us (0.973)
  local copies, waits for them, and re-layouts: 3.01 us -> 0 us
    unnamed x8 -> x0, local copies, waits for them, and re-layouts: 3.01 us -> none
    pallas_call x1, Pallas kernels: 11.8 us -> 12.9 us  [scatter(): pl.pallas_call(functools.partial(scatter_kernel, slot_count), out_shape=j...]
where the time goes in v4:
time: 107 us
  Pallas kernels  107 us (100%)
    pallas_call x1, Pallas kernels, step(): pl.pallas_call(functools.partial(step_kernel, slot_count, table_size, gro...  93.9 us
    pallas_call x1, Pallas kernels, scatter(): pl.pallas_call(functools.partial(scatter_kernel, slot_count), out_shape=j...  12.9 us

profile of v4, /device:TPU:1, one launch (start us, length us, event | category | flops | bytes accessed | tf_op | source)
XLA Modules:
  0.0 107.0 jit_solution(7255094486717358449)
XLA Ops:
  0.0 93.9 %step.1 = (f32[16,8,128]{2,1,0:T(8,128)}, s16[128,8,512]{2,1,0:T(8,128)(2,1)}, f32[4,32,400]{2,1,0:T(8,128)}) custom-call(s32[2,1,256]{2,1,0:T(1,128)} %bitcast.19, s32[2,256]{1,0:T(2,128)} %bitcast.20, s32[1,32]{1,0:T(1,128)} %bitcast.17, s32[3,256]{1,0:T(4,128)} %bitcast.16, s32[1,256]{1,0:T(1,128)} %bitcast.21, bf16[400,4096]{1,0:T(8,128)(2,1)} %bitcast.13, ...), custom_call_target="tpu_custom_call" | custom-call | tf_op jit(solution)/shard_map/step/pallas_call | solution.py:529
  93.9 12.9 %scatter.1 = f32[400,4096]{1,0:T(8,128)} custom-call(f32[128,128]{1,0:T(8,128)} %bitcast.15, s32[1,32]{1,0:T(1,128)} %bitcast.18, s16[1024,512]{1,0:T(8,128)(2,1)} %bitcast.14, f32[4,32,400]{2,1,0:T(8,128)} %get-tuple-element.10.pool_hbm), custom_call_target="tpu_custom_call" | custom-call | tf_op jit(solution)/shard_map/scatter/pallas_call | solution.py:590

commit v5 on v4

--- a/solution.py
+++ b/solution.py
@@ -72,8 +72,11 @@
     def over(value, size):
         return lax.div(value, jnp.full_like(value, size))
 
-    core, depth, rest = part(position, 2), part(over(position, 2), 4), over(position, 8)
-    line, plane = part(rest, 4), over(rest, 4)
+    if isinstance(position, int):
+        core, depth, line, plane = position % 2, position // 2 % 4, position // 8 % 4, position // 32
+    else:
+        core, depth, rest = part(position, 2), part(over(position, 2), 4), over(position, 8)
+        line, plane = part(rest, 4), over(rest, 4)
     y = part(over(row_me, 2) + line + depth, 4)
     x = part(over(row_me, 8) + plane + depth + 2 * line, 4)
     core = part(row_me + core, 2)
@@ -258,19 +261,19 @@
     )
     quarter = devices // 4
 
-    def send_rows(i, _):
+    def send_rows(i):
         pltpu.make_async_remote_copy(
             src_ref=served.at[i], dst_ref=back_ref.at[me],
             send_sem=row_send, recv_sem=row_recv,
             device_id=partner(i, row_me, col_me), device_id_type=MESH,
         ).start()
-        return 0
 
     for part in (1, 2, 3, 0):
         size = quarter * slot_count
         rows = rows_at(column[part * size : (part + 1) * size, :])
         served[part * quarter : (part + 1) * quarter] = rows.reshape(quarter, slot_count, width)
-        lax.fori_loop(max(1, part * quarter), (part + 1) * quarter, send_rows, 0)
+        for i in range(max(1, part * quarter), (part + 1) * quarter):
+            send_rows(i)
 
     back_ref[me] = served[0]
     relations_part(1)
@@ -432,13 +435,12 @@
     slot_count = rows // devices
     quarter = devices // 4
 
-    def send_rows(i, _):
+    def send_rows(i):
         pltpu.make_async_remote_copy(
             src_ref=coded.at[i], dst_ref=returned_ref.at[me],
             send_sem=row_send, recv_sem=row_recv,
             device_id=partner(i, row_me, col_me), device_id_type=MESH,
         ).start()
-        return 0
 
     for part in range(4):
         size = quarter * slot_count
@@ -454,7 +456,8 @@
         coded[part * quarter : (part + 1) * quarter] = level.reshape(
             quarter, slot_count, codes.shape[0]
         )
-        lax.fori_loop(max(1, part * quarter), (part + 1) * quarter, send_rows, 0)
+        for i in range(max(1, part * quarter), (part + 1) * quarter):
+            send_rows(i)
 
     returned_ref[me] = coded[0]
     pool_ref[0] = pool_rows[0]

time: 107 us -> 107 us (level)
  no operation moved by 1% of the time
where the time goes in v5:
time: 107 us
  Pallas kernels  106 us (99%)
    pallas_call x1, Pallas kernels, step(): pl.pallas_call(functools.partial(step_kernel, slot_count, table_size, gro...  93.5 us
    pallas_call x1, Pallas kernels, scatter(): pl.pallas_call(functools.partial(scatter_kernel, slot_count), out_shape=j...  12.9 us

profile of v5, /device:TPU:1, one launch (start us, length us, event | category | flops | bytes accessed | tf_op | source)
XLA Modules:
  0.0 106.5 jit_solution(17157900396171273674)
XLA Ops:
  0.0 93.5 %step.1 = (f32[16,8,128]{2,1,0:T(8,128)}, s16[128,8,512]{2,1,0:T(8,128)(2,1)}, f32[4,32,400]{2,1,0:T(8,128)}) custom-call(s32[2,1,256]{2,1,0:T(1,128)} %bitcast.19, s32[2,256]{1,0:T(2,128)} %bitcast.20, s32[1,32]{1,0:T(1,128)} %bitcast.17, s32[3,256]{1,0:T(4,128)} %bitcast.16, s32[1,256]{1,0:T(1,128)} %bitcast.21, bf16[400,4096]{1,0:T(8,128)(2,1)} %bitcast.13, ...), custom_call_target="tpu_custom_call" | custom-call | tf_op jit(solution)/shard_map/step/pallas_call | solution.py:532
  93.5 12.9 %scatter.1 = f32[400,4096]{1,0:T(8,128)} custom-call(f32[128,128]{1,0:T(8,128)} %bitcast.15, s32[1,32]{1,0:T(1,128)} %bitcast.18, s16[1024,512]{1,0:T(8,128)(2,1)} %bitcast.14, f32[4,32,400]{2,1,0:T(8,128)} %get-tuple-element.10.pool_hbm), custom_call_target="tpu_custom_call" | custom-call | tf_op jit(solution)/shard_map/scatter/pallas_call | solution.py:593
